TPU v7x, 512 devices: a whole 4x8x8 slice. The times are simulated.
512 devices in a mesh: comp: 32 (over z, y_hi), seq: 16 (over x, y_lo, core).
Axes of the slice: x: 4, y: 8 (y_hi: 4, y_lo: 2; y = y_hi * 2 + y_lo), z: 8, core: 2. Of those that a mesh axis runs over, the one named last changes fastest.
Arguments:
- queries: bfloat16 [32, 2048, 4096], P('comp', 'seq'), may hold values from -24 to 24
- keys: bfloat16 [32, 2048, 4096], P('comp', 'seq'), may hold values from -24 to 24
- values: bfloat16 [32, 2048, 4096], P('comp', 'seq'), may hold values from -6 to 6
- latent: float32 [64, 2048], P('comp', 'seq'), may hold values from -6 to 6
- prev_denoised: float32 [64, 2048], P('comp', 'seq'), may hold values from -6 to 6
- head_weight: bfloat16 [4096, 64], P('seq'), may hold values from -0.09375 to 0.09375
Outputs:
- hidden: bfloat16 [32, 2048, 4096], P('comp', 'seq')
- new_latent: float32 [64, 2048], P('comp', 'seq')
- denoised: float32 [64, 2048], P('comp', 'seq')
All inputs are finite; a program needn't handle non-finite values.
Results may differ from a plain program's by a relative error of at most 0.008.
Values may be sent and summed in bfloat16 or wider, within the bound.
No kernel may reach another device: no remote copies, remote signals or barrier semaphores. Data moves between devices by JAX's collectives and lax.ppermute only.
A program may use at most 64 MiB of HBM per device.

v0:
```python
import math

import jax
import jax.numpy as jnp
from jax import lax
from jax.sharding import PartitionSpec as P

HD = 128


alpha_now = 0.6
sigma_now = 0.8
alpha_next = 0.8
sigma_next = 0.6
step_before = 0.4


def broadcast(block, axis, source):
    block = jnp.where(lax.axis_index(axis) == source, block, jnp.zeros_like(block))
    return lax.psum(block, axis)


def group_attention(query_grp, key_grp, value_grp):
    length = query_grp.shape[0]
    block = math.gcd(length, 512)
    scale = query_grp.shape[2] ** (-0.5)

    def one_block(query_block):
        scores = (
            jnp.einsum("qgd,kgd->gqk", query_block, key_grp, preferred_element_type=jnp.float32)
            * scale
        )
        highest = jnp.max(scores, axis=2, keepdims=True)
        weights = jnp.exp(scores - highest)
        totals = jnp.sum(weights, axis=2, keepdims=True)
        probs = (weights / totals).astype(jnp.bfloat16)
        return jnp.einsum(
            "gqk,kgd->qgd", probs, value_grp, preferred_element_type=jnp.float32
        ).astype(jnp.bfloat16)

    blocks = query_grp.reshape(length // block, block, query_grp.shape[1], query_grp.shape[2])
    return lax.map(one_block, blocks).reshape(query_grp.shape)


def on_device(queries, keys, values, latent, prev_denoised, head_weight):
    seq_count = lax.axis_size("seq")
    local_tokens = queries.shape[1]
    width = queries.shape[2]
    per_device = width // HD // seq_count
    grouped_shape = (local_tokens, seq_count, per_device, HD)
    query_tok = queries[0].reshape(grouped_shape)
    key_tok = keys[0].reshape(grouped_shape)
    value_tok = values[0].reshape(grouped_shape)
    query_heads, key_heads, value_heads = (
        lax.all_to_all(query_tok, "seq", split_axis=1, concat_axis=0, tiled=True),
        lax.all_to_all(key_tok, "seq", split_axis=1, concat_axis=0, tiled=True),
        lax.all_to_all(value_tok, "seq", split_axis=1, concat_axis=0, tiled=True),
    )
    head_layout = group_attention(query_heads[:, 0], key_heads[:, 0], value_heads[:, 0])[:, None]
    returned = lax.all_to_all(head_layout, "seq", split_axis=0, concat_axis=1, tiled=True)
    hidden_tok = returned.reshape(local_tokens, width)
    squares = jnp.sum(jnp.square(hidden_tok.astype(jnp.float32)), axis=1)
    projected = jnp.dot(
        hidden_tok,
        lax.all_gather(head_weight, "seq", axis=0, tiled=True),
        preferred_element_type=jnp.float32,
    )
    norm_root = jnp.sqrt(squares / width + 1e-06)
    noise_all = (projected / norm_root[:, None]).T
    comp_count = lax.axis_size("comp")
    own_channels = latent.shape[0]
    position = lax.axis_index("comp")
    everyone = broadcast(noise_all.astype(jnp.bfloat16), "comp", comp_count - 1).astype(
        noise_all.dtype
    )
    noise_own = lax.dynamic_slice_in_dim(everyone, position * own_channels, own_channels, 0)
    denoised = (latent - sigma_now * noise_own) / alpha_now
    step_now = math.log(alpha_next / sigma_next) - math.log(alpha_now / sigma_now)
    ratio = step_before / step_now
    blend = (1.0 + 0.5 / ratio) * denoised - 0.5 / ratio * prev_denoised
    new_latent = sigma_next / sigma_now * latent - alpha_next * (math.exp(-step_now) - 1.0) * blend
    return (hidden_tok[None], new_latent, denoised)


def solution(mesh):
    return jax.shard_map(
        on_device,
        mesh=mesh,
        in_specs=(
            P("comp", "seq", None),
            P("comp", "seq", None),
            P("comp", "seq", None),
            P("comp", "seq"),
            P("comp", "seq"),
            P("seq", None),
        ),
        out_specs=(P("comp", "seq", None), P("comp", "seq"), P("comp", "seq")),
        check_vma=False,
    )
```

profile of v0, /device:TPU:8, one launch (start us, length us, event | category | flops | bytes accessed | tf_op | source)
XLA Modules:
  0.0 317.8 jit_solution(8267672061850431944)
XLA Ops:
  0.6 2.3 copy.33
  2.9 9.3 %all-to-all-start = ((bf16[128,16,2,128]{0,3,2,1:T(8,128)(2,1)}), bf16[128,16,2,128]{0,3,2,1:T(8,128)(2,1)S(1)}, u32[]{:S(2)}, u32[]{:S(2)}) async-start(bf16[128,16,2,128]{0,3,2,1:T(8,128)(2,1)} %bitcast.3), calls=%async_computation | async-start | bytes 2097152 | tf_op jit(solution)/shard_map/all_to_all | solution.py:55
  12.2 1.6 copy.35
  13.8 1.3 copy.36
  15.1 12.5 %all-to-all-done = bf16[128,16,2,128]{0,3,2,1:T(8,128)(2,1)S(1)} async-done(((bf16[128,16,2,128]{0,3,2,1:T(8,128)(2,1)}), bf16[128,16,2,128]{0,3,2,1:T(8,128)(2,1)S(1)}, u32[]{:S(2)}, u32[]{:S(2)}) %all-to-all-start) | async-done | bytes 1048608 | tf_op jit(solution)/shard_map/all_to_all | solution.py:55
  27.6 4.8 %all-to-all-start.1 = ((bf16[128,16,2,128]{3,0,2,1:T(8,128)(2,1)}), bf16[128,16,2,128]{3,0,2,1:T(8,128)(2,1)S(1)}, u32[]{:S(2)}, u32[]{:S(2)}) async-start(bf16[128,16,2,128]{3,0,2,1:T(8,128)(2,1)} %copy.36), calls=%async_computation.1 | async-start | bytes 2097152 | tf_op jit(solution)/shard_map/all_to_all | solution.py:56
  32.4 1.6 copy.38
  34.0 1.3 copy.39
  35.3 12.5 %all-to-all-done.1 = bf16[128,16,2,128]{3,0,2,1:T(8,128)(2,1)S(1)} async-done(((bf16[128,16,2,128]{3,0,2,1:T(8,128)(2,1)}), bf16[128,16,2,128]{3,0,2,1:T(8,128)(2,1)S(1)}, u32[]{:S(2)}, u32[]{:S(2)}) %all-to-all-start.1) | async-done | bytes 1048608 | tf_op jit(solution)/shard_map/all_to_all | solution.py:56
  47.8 4.8 %all-to-all-start.2 = ((bf16[128,16,2,128]{3,0,2,1:T(8,128)(2,1)}), bf16[128,16,2,128]{3,0,2,1:T(8,128)(2,1)S(1)}, u32[]{:S(2)}, u32[]{:S(2)}) async-start(bf16[128,16,2,128]{3,0,2,1:T(8,128)(2,1)} %copy.39), calls=%async_computation.2 | async-start | bytes 2097152 | tf_op jit(solution)/shard_map/all_to_all | solution.py:57
  52.6 1.4 copy.34
  54.0 0.1 copy.37
  54.1 13.9 %all-to-all-done.2 = bf16[128,16,2,128]{3,0,2,1:T(8,128)(2,1)S(1)} async-done(((bf16[128,16,2,128]{3,0,2,1:T(8,128)(2,1)}), bf16[128,16,2,128]{3,0,2,1:T(8,128)(2,1)S(1)}, u32[]{:S(2)}, u32[]{:S(2)}) %all-to-all-start.2) | async-done | bytes 1048608 | tf_op jit(solution)/shard_map/all_to_all | solution.py:57
  68.0 0.1 copy.40
  68.1 0.0 copy-start
  68.1 48.6 %while.10 = (s32[]{:T(128)}, bf16[4,512,2,128]{3,1,0,2:T(8,128)(2,1)}, bf16[4,512,2,128]{3,1,0,2:T(8,128)(2,1)}, bf16[2048,2,128]{2,0,1:T(8,128)(2,1)S(1)}, bf16[2048,2,128]{2,0,1:T(8,128)(2,1)S(1)}, /*index=5*/s32[]{:T(128)}) while((s32[]{:T(128)}, bf16[4,512,2,128]{3,1,0,2:T(8,128)(2,1)}, bf16[4,512,2,128]{3,1,0,2:T(8,128)(2,1)}, ...), condition=%wide.region_3.4_spmd, body=%wide.region_0.3_spmd.sunk | while | flops 1084360704 | bytes 19406932 | solution.py:42
  68.2 6.8 %fusion.48 = (f32[2,512]{1,0:T(2,128)S(1)}, f32[2,512,2048]{2,1,0:T(8,128)}) fusion(bf16[2048,2,128]{2,0,1:T(8,128)(2,1)S(1)} %get-tuple-element.124, bf16[4,512,2,128]{3,1,0,2:T(8,128)(2,1)} %get-tuple-element.123, s32[]{:T(128)S(6)} %copy.54), kind=kOutput, calls=%fused_computation.28.clone.1 | convolution fusion | flops 543164416 | bytes 9703428 | tf_op jit(solution)/shard_map/while/body/eval_jaxpr/sub | solution.py:34
  74.9 5.4 %fusion.49 = bf16[4,512,2,128]{3,1,0,2:T(8,128)(2,1)} fusion(bf16[4,512,2,128]{3,1,0,2:T(8,128)(2,1)} %get-tuple-element.116, s32[]{:T(128)S(6)} %copy.54, bf16[2048,2,128]{2,0,1:T(8,128)(2,1)S(1)} %get-tuple-element.125, f32[2,512,2048]{2,1,0:T(8,128)} %get-tuple-element.107, f32[2,512]{1,0:T(2,128)S(1)} %get-tuple-element.108), kind=kOutput, calls=%fused_computation.9.clone.1 | convolution fusion | flops 541196288 | bytes 9703428 | tf_op jit(solution)/shard_map/while/body/eval_jaxpr/gqk,kgd->qgd/dot_general | solution.py:37
  80.3 6.8 %fusion.48 = (f32[2,512]{1,0:T(2,128)S(1)}, f32[2,512,2048]{2,1,0:T(8,128)}) fusion(bf16[2048,2,128]{2,0,1:T(8,128)(2,1)S(1)} %get-tuple-element.124, bf16[4,512,2,128]{3,1,0,2:T(8,128)(2,1)} %get-tuple-element.123, s32[]{:T(128)S(6)} %copy.54), kind=kOutput, calls=%fused_computation.28.clone.1 | convolution fusion | flops 543164416 | bytes 9703428 | tf_op jit(solution)/shard_map/while/body/eval_jaxpr/sub | solution.py:34
  87.1 5.4 %fusion.49 = bf16[4,512,2,128]{3,1,0,2:T(8,128)(2,1)} fusion(bf16[4,512,2,128]{3,1,0,2:T(8,128)(2,1)} %get-tuple-element.116, s32[]{:T(128)S(6)} %copy.54, bf16[2048,2,128]{2,0,1:T(8,128)(2,1)S(1)} %get-tuple-element.125, f32[2,512,2048]{2,1,0:T(8,128)} %get-tuple-element.107, f32[2,512]{1,0:T(2,128)S(1)} %get-tuple-element.108), kind=kOutput, calls=%fused_computation.9.clone.1 | convolution fusion | flops 541196288 | bytes 9703428 | tf_op jit(solution)/shard_map/while/body/eval_jaxpr/gqk,kgd->qgd/dot_general | solution.py:37
  92.4 6.8 %fusion.48 = (f32[2,512]{1,0:T(2,128)S(1)}, f32[2,512,2048]{2,1,0:T(8,128)}) fusion(bf16[2048,2,128]{2,0,1:T(8,128)(2,1)S(1)} %get-tuple-element.124, bf16[4,512,2,128]{3,1,0,2:T(8,128)(2,1)} %get-tuple-element.123, s32[]{:T(128)S(6)} %copy.54), kind=kOutput, calls=%fused_computation.28.clone.1 | convolution fusion | flops 543164416 | bytes 9703428 | tf_op jit(solution)/shard_map/while/body/eval_jaxpr/sub | solution.py:34
  99.2 5.4 %fusion.49 = bf16[4,512,2,128]{3,1,0,2:T(8,128)(2,1)} fusion(bf16[4,512,2,128]{3,1,0,2:T(8,128)(2,1)} %get-tuple-element.116, s32[]{:T(128)S(6)} %copy.54, bf16[2048,2,128]{2,0,1:T(8,128)(2,1)S(1)} %get-tuple-element.125, f32[2,512,2048]{2,1,0:T(8,128)} %get-tuple-element.107, f32[2,512]{1,0:T(2,128)S(1)} %get-tuple-element.108), kind=kOutput, calls=%fused_computation.9.clone.1 | convolution fusion | flops 541196288 | bytes 9703428 | tf_op jit(solution)/shard_map/while/body/eval_jaxpr/gqk,kgd->qgd/dot_general | solution.py:37
  104.6 6.8 %fusion.48 = (f32[2,512]{1,0:T(2,128)S(1)}, f32[2,512,2048]{2,1,0:T(8,128)}) fusion(bf16[2048,2,128]{2,0,1:T(8,128)(2,1)S(1)} %get-tuple-element.124, bf16[4,512,2,128]{3,1,0,2:T(8,128)(2,1)} %get-tuple-element.123, s32[]{:T(128)S(6)} %copy.54), kind=kOutput, calls=%fused_computation.28.clone.1 | convolution fusion | flops 543164416 | bytes 9703428 | tf_op jit(solution)/shard_map/while/body/eval_jaxpr/sub | solution.py:34
  111.3 5.4 %fusion.49 = bf16[4,512,2,128]{3,1,0,2:T(8,128)(2,1)} fusion(bf16[4,512,2,128]{3,1,0,2:T(8,128)(2,1)} %get-tuple-element.116, s32[]{:T(128)S(6)} %copy.54, bf16[2048,2,128]{2,0,1:T(8,128)(2,1)S(1)} %get-tuple-element.125, f32[2,512,2048]{2,1,0:T(8,128)} %get-tuple-element.107, f32[2,512]{1,0:T(2,128)S(1)} %get-tuple-element.108), kind=kOutput, calls=%fused_computation.9.clone.1 | convolution fusion | flops 541196288 | bytes 9703428 | tf_op jit(solution)/shard_map/while/body/eval_jaxpr/gqk,kgd->qgd/dot_general | solution.py:37
  116.7 0.0 copy-start.1
  116.7 0.0 copy-start.2
  116.7 3.6 %copy.43 = bf16[2048,1,2,128]{3,2,1,0:T(2,128)(2,1)} copy(bf16[2048,1,2,128]{3,0,2,1:T(8,128)(2,1)} %bitcast.71) | data formatting | bytes 2097152 | tf_op jit(solution)/shard_map/broadcast_in_dim;reshape | solution.py:59
  120.4 4.8 %all-to-all-start.3 = ((bf16[2048,1,2,128]{3,2,1,0:T(2,128)(2,1)}), bf16[2048,1,2,128]{3,2,1,0:T(2,128)(2,1)S(1)}, u32[]{:S(2)}, u32[]{:S(2)}) async-start(bf16[2048,1,2,128]{3,2,1,0:T(2,128)(2,1)} %copy.43), calls=%async_computation.3 | async-start | bytes 2097152 | tf_op jit(solution)/shard_map/all_to_all | solution.py:60
  125.2 0.0 copy-done
  125.2 28.9 %all_gather.3 = bf16[4096,64]{0,1:T(8,128)(2,1)S(1)} all-gather(bf16[256,64]{0,1:T(8,128)(2,1)S(1)} %copy-done), channel_id=1, replica_groups=mesh['comp'=32,'seq'=16] {'seq'}, dimensions={0}, use_global_device_ids=true | all-gather | bytes 557056 | tf_op jit(solution)/shard_map/all_gather | solution.py:65
  154.1 0.0 all-to-all-done.3
  154.1 0.1 copy.44
  154.2 0.7 copy.45
  154.9 0.3 multiply_reduce_fusion.1
  155.2 1.3 copy.47
  156.5 0.3 fusion.29
  156.8 160.4 %psum.7 = bf16[64,128]{1,0:T(8,128)(2,1)S(1)} all-reduce(bf16[64,128]{1,0:T(8,128)(2,1)S(1)} %fusion.29), channel_id=1, replica_groups=mesh['comp'=32,'seq'=16] {'comp'}, use_global_device_ids=true, to_apply=%region_5.6 | all-reduce | flops 8192 | bytes 32768 | tf_op jit(solution)/shard_map/psum | solution.py:20
  317.2 0.0 copy-done.1
  317.2 0.0 copy-done.2
  317.2 0.6 broadcast_multiply_fusion
  (2 shorter events, 0.0 us)
Async XLA Ops:
  2.9 24.7 %all-to-all-start = ((bf16[128,16,2,128]{0,3,2,1:T(8,128)(2,1)}), bf16[128,16,2,128]{0,3,2,1:T(8,128)(2,1)S(1)}, u32[]{:S(2)}, u32[]{:S(2)}) async-start(bf16[128,16,2,128]{0,3,2,1:T(8,128)(2,1)} %bitcast.3), calls=%async_computation | async-start | bytes 2097152 | tf_op jit(solution)/shard_map/all_to_all | solution.py:55
  27.6 20.2 %all-to-all-start.1 = ((bf16[128,16,2,128]{3,0,2,1:T(8,128)(2,1)}), bf16[128,16,2,128]{3,0,2,1:T(8,128)(2,1)S(1)}, u32[]{:S(2)}, u32[]{:S(2)}) async-start(bf16[128,16,2,128]{3,0,2,1:T(8,128)(2,1)} %copy.36), calls=%async_computation.1 | async-start | bytes 2097152 | tf_op jit(solution)/shard_map/all_to_all | solution.py:56
  47.8 20.2 %all-to-all-start.2 = ((bf16[128,16,2,128]{3,0,2,1:T(8,128)(2,1)}), bf16[128,16,2,128]{3,0,2,1:T(8,128)(2,1)S(1)}, u32[]{:S(2)}, u32[]{:S(2)}) async-start(bf16[128,16,2,128]{3,0,2,1:T(8,128)(2,1)} %copy.39), calls=%async_computation.2 | async-start | bytes 2097152 | tf_op jit(solution)/shard_map/all_to_all | solution.py:57
  68.1 57.1 %copy-start = (bf16[256,64]{0,1:T(8,128)(2,1)S(1)}, bf16[256,64]{0,1:T(8,128)(2,1)}, u32[]{:S(2)}) copy-start(bf16[256,64]{0,1:T(8,128)(2,1)} %param.13) | copy-start | bytes 98308
  116.7 200.5 %copy-start.1 = (f32[2,128]{1,0:T(2,128)S(1)}, f32[2,128]{1,0:T(2,128)}, u32[]{:S(2)}) copy-start(f32[2,128]{1,0:T(2,128)} %param.11) | copy-start | bytes 3076
  116.7 200.5 %copy-start.2 = (f32[2,128]{1,0:T(2,128)S(1)}, f32[2,128]{1,0:T(2,128)}, u32[]{:S(2)}) copy-start(f32[2,128]{1,0:T(2,128)} %param.12) | copy-start | bytes 3076
  120.4 33.7 %all-to-all-start.3 = ((bf16[2048,1,2,128]{3,2,1,0:T(2,128)(2,1)}), bf16[2048,1,2,128]{3,2,1,0:T(2,128)(2,1)S(1)}, u32[]{:S(2)}, u32[]{:S(2)}) async-start(bf16[2048,1,2,128]{3,2,1,0:T(2,128)(2,1)} %copy.43), calls=%async_computation.3 | async-start | bytes 2097152 | tf_op jit(solution)/shard_map/all_to_all | solution.py:60
where the time goes:
time: 319 us; the launch traced here: 318 us
  blocking collectives  189 us (59%)
  matrix products  48.9 us (15%)
  waiting for transfers between devices  38.8 us (12%)
  starting transfers between devices  23.8 us (7%)
  local copies, waits for them, and re-layouts  15.4 us (5%)
    psum x1, blocking collectives, broadcast(): return lax.psum(block, axis)  160 us
    all_gather x1, blocking collectives, on_device(): lax.all_gather(head_weight, 'seq', axis=0, tiled=True)  28.9 us
    sub x4, matrix products, one_block(): weights = jnp.exp(scores - highest)  27 us
    dot_general x4, matrix products, one_block(): jnp.einsum('gqk,kgd->qgd', probs, value_grp, preferred_element_type=jnp.f...  21.5 us
    all_to_all x1, waiting for transfers between devices, on_device(): lax.all_to_all(value_tok, 'seq', split_axis=1, concat_axis=0, tiled=True)  13.9 us
    all_to_all x1, waiting for transfers between devices, on_device(): lax.all_to_all(key_tok, 'seq', split_axis=1, concat_axis=0, tiled=True)  12.5 us
    all_to_all x1, waiting for transfers between devices, on_device(): lax.all_to_all(query_tok, 'seq', split_axis=1, concat_axis=0, tiled=True)  12.5 us
    all_to_all x1, starting transfers between devices, on_device(): lax.all_to_all(query_tok, 'seq', split_axis=1, concat_axis=0, tiled=True)  9.27 us
  transfers between devices with their start and end apart: 4, of which 3 were waited for; matrix products, arithmetic and copies ran while one was open for 2% of the time, Pallas kernels for 0%

commit v1 on v0

v1 whole, which is shorter than its diff:
```python
import math

import jax
import jax.numpy as jnp
from jax import lax
from jax.experimental import pallas as pl
from jax.experimental.pallas import tpu as pltpu
from jax.sharding import PartitionSpec as P

HD = 128
BLOCK = 256

alpha_now = 0.6
sigma_now = 0.8
alpha_next = 0.8
sigma_next = 0.6
step_before = 0.4


def pack(queries, keys, values, seq_count):
    tokens, width = queries.shape
    cols = width // seq_count

    def kernel(q_ref, k_ref, v_ref, out_ref, sem):
        copies = []
        for n, ref in enumerate((q_ref, k_ref, v_ref)):
            for d in range(seq_count):
                copies.append(
                    pltpu.make_async_copy(ref.at[:, pl.ds(d * cols, cols)], out_ref.at[d, n], sem.at[n, d])
                )
        for copy in copies:
            copy.start()
        for copy in copies:
            copy.wait()

    return pl.pallas_call(
        kernel,
        out_shape=jax.ShapeDtypeStruct((seq_count, 3, tokens, cols), queries.dtype),
        in_specs=[pl.BlockSpec(memory_space=pl.ANY)] * 3,
        out_specs=pl.BlockSpec(memory_space=pl.ANY),
        scratch_shapes=[pltpu.SemaphoreType.DMA((3, seq_count))],
        name="pack",
    )(queries, keys, values)


def attention(blocks):
    seq_count, _, tokens, cols = blocks.shape
    length = seq_count * tokens
    heads = cols // HD
    group = BLOCK // tokens
    scale = HD ** (-0.5) * math.log2(math.e)

    def kernel(in_ref, out_ref, key_wide, value_wide):
        for h in range(heads):
            head = slice(h * HD, (h + 1) * HD)
            key = in_ref[:, 1, :, head].reshape(length, HD)
            key_wide[h, :, :HD] = key
            key_wide[h, :, HD:] = key
            value_wide[h, :, :HD] = in_ref[:, 2, :, head].reshape(length, HD)
            value_wide[h, :, HD:] = jnp.ones((length, HD), jnp.bfloat16)
        for h in range(heads):
            head = slice(h * HD, (h + 1) * HD)
            for b in range(0, seq_count, group):
                query = in_ref[b : b + group, 0, :, head].reshape(BLOCK, HD).astype(jnp.float32) * scale
                high = query.astype(jnp.bfloat16)
                low = (query - high.astype(jnp.float32)).astype(jnp.bfloat16)
                scores = lax.dot_general(
                    jnp.concatenate([high, low], axis=1),
                    key_wide[h],
                    (((1,), (1,)), ((), ())),
                    preferred_element_type=jnp.float32,
                )
                weights = jnp.exp2(scores - jnp.max(scores, axis=1, keepdims=True)).astype(jnp.bfloat16)
                sums = jnp.dot(weights, value_wide[h], preferred_element_type=jnp.float32)
                result = sums[:, :HD] / sums[:, HD:]
                out_ref[b : b + group, :, head] = result.astype(jnp.bfloat16).reshape(group, tokens, HD)

    return pl.pallas_call(
        kernel,
        out_shape=jax.ShapeDtypeStruct((seq_count, tokens, cols), jnp.bfloat16),
        in_specs=[pl.BlockSpec(memory_space=pltpu.VMEM)],
        out_specs=pl.BlockSpec(memory_space=pltpu.VMEM),
        scratch_shapes=[
            pltpu.VMEM((heads, length, 2 * HD), jnp.bfloat16),
            pltpu.VMEM((heads, length, 2 * HD), jnp.bfloat16),
        ],
        compiler_params=pltpu.CompilerParams(vmem_limit_bytes=56 * 1024 * 1024),
        name="attention",
    )(blocks)


def project(returned, weight, comp_count):
    seq_count, tokens, cols = returned.shape
    width, channels = weight.shape
    own = channels // comp_count

    def kernel(in_ref, weight_ref, hidden_ref, noise_ref):
        total = jnp.zeros((tokens, channels), jnp.float32)
        squares = jnp.zeros((tokens, cols), jnp.float32)
        for d in range(seq_count):
            part = in_ref[d]
            hidden_ref[:, d * cols : (d + 1) * cols] = part
            squares += jnp.square(part.astype(jnp.float32))
            total += jnp.dot(part, weight_ref[d * cols : (d + 1) * cols, :], preferred_element_type=jnp.float32)
        root = jnp.sqrt(jnp.sum(squares, axis=1, keepdims=True) / width + 1e-06)
        noise = jnp.concatenate([total / root] * (tokens // channels), axis=1).T
        noise_ref[...] = jnp.zeros(noise_ref.shape, jnp.float32)
        for c in range(comp_count):
            noise_ref[c, :own, :] = noise[c * own : (c + 1) * own, :]

    return pl.pallas_call(
        kernel,
        out_shape=(
            jax.ShapeDtypeStruct((tokens, width), jnp.bfloat16),
            jax.ShapeDtypeStruct((comp_count, 8, tokens), jnp.float32),
        ),
        in_specs=[pl.BlockSpec(memory_space=pltpu.VMEM)] * 2,
        out_specs=(pl.BlockSpec(memory_space=pltpu.VMEM),) * 2,
        compiler_params=pltpu.CompilerParams(vmem_limit_bytes=56 * 1024 * 1024),
        name="project",
    )(returned, weight)


def on_device(queries, keys, values, latent, prev_denoised, head_weight):
    seq_count = lax.axis_size("seq")
    comp_count = lax.axis_size("comp")
    own_channels = latent.shape[0]
    packed = pack(queries[0], keys[0], values[0], seq_count)
    blocks = lax.all_to_all(packed, "seq", split_axis=0, concat_axis=0, tiled=True)
    weight = lax.all_gather(head_weight, "seq", axis=0, tiled=True)
    outputs = attention(blocks)
    returned = lax.all_to_all(outputs, "seq", split_axis=0, concat_axis=0, tiled=True)
    hidden, noise = project(returned, weight, comp_count)
    everyone = lax.all_to_all(noise, "comp", split_axis=0, concat_axis=0, tiled=True)
    noise_own = everyone[comp_count - 1, :own_channels]
    denoised = (latent - sigma_now * noise_own) / alpha_now
    step_now = math.log(alpha_next / sigma_next) - math.log(alpha_now / sigma_now)
    ratio = step_before / step_now
    blend = (1.0 + 0.5 / ratio) * denoised - 0.5 / ratio * prev_denoised
    new_latent = sigma_next / sigma_now * latent - alpha_next * (math.exp(-step_now) - 1.0) * blend
    return (hidden[None], new_latent, denoised)


def solution(mesh):
    return jax.shard_map(
        on_device,
        mesh=mesh,
        in_specs=(
            P("comp", "seq", None),
            P("comp", "seq", None),
            P("comp", "seq", None),
            P("comp", "seq"),
            P("comp", "seq"),
            P("seq", None),
        ),
        out_specs=(P("comp", "seq", None), P("comp", "seq"), P("comp", "seq")),
        check_vma=False,
    )
```

time: 319 us -> 225 us (0.71)
  the two profiles are of different devices: /device:TPU:8 before, /device:TPU:1 now
where the time goes in v1:
time: 225 us
  Pallas kernels  113 us (50%)
  blocking collectives  105 us (47%)
  starting transfers between devices  4.74 us (2%)
    pallas_call x1, Pallas kernels, pack(): pl.pallas_call(kernel, out_shape=jax.ShapeDtypeStruct((seq_count, 3, toke...  96.8 us
    all_to_all x1, blocking collectives, on_device(): lax.all_to_all(packed, 'seq', split_axis=0, concat_axis=0, tiled=True)  49.2 us
    all_gather x1, blocking collectives, on_device(): weight = lax.all_gather(head_weight, 'seq', axis=0, tiled=True)  34 us
    all_to_all x1, blocking collectives, on_device(): lax.all_to_all(noise, 'comp', split_axis=0, concat_axis=0, tiled=True)  21.8 us
    pallas_call x1, Pallas kernels, attention(): pl.pallas_call(kernel, out_shape=jax.ShapeDtypeStruct((seq_count, tokens,...  13 us
    all_to_all x1, starting transfers between devices, on_device(): lax.all_to_all(outputs, 'seq', split_axis=0, concat_axis=0, tiled=True)  4.74 us
  transfers between devices with their start and end apart: 1, of which 0 were waited for; matrix products, arithmetic and copies ran while one was open for 0% of the time, Pallas kernels for 0%

profile of v1, /device:TPU:1, one launch (start us, length us, event | category | flops | bytes accessed | tf_op | source)
XLA Modules:
  0.0 224.6 jit_solution(8157208870214354646)
XLA Ops:
  0.6 96.8 %pack.1 = bf16[16,3,128,256]{3,2,1,0:T(8,128)(2,1)} custom-call(bf16[128,4096]{1,0:T(8,128)(2,1)} %bitcast.12, bf16[128,4096]{1,0:T(8,128)(2,1)} %bitcast.13, bf16[128,4096]{1,0:T(8,128)(2,1)} %bitcast.14), custom_call_target="tpu_custom_call" | custom-call | tf_op jit(solution)/shard_map/pack/pallas_call | solution.py:36
  97.5 49.2 %all_to_all.15.in_ref = bf16[16,3,128,256]{3,2,1,0:T(8,128)(2,1)} all-to-all(bf16[16,3,128,256]{3,2,1,0:T(8,128)(2,1)} %pack.1), channel_id=1, replica_groups=mesh['comp'=32,'seq'=16] {'seq'}, dimensions={0} | all-to-all | bytes 6291456 | tf_op jit(solution)/shard_map/all_to_all | solution.py:129
  146.6 0.0 copy-start.1
  146.6 13.0 %attention.1 = bf16[16,128,256]{2,1,0:T(8,128)(2,1)} custom-call(bf16[16,3,128,256]{3,2,1,0:T(8,128)(2,1)} %all_to_all.15.in_ref), custom_call_target="tpu_custom_call" | custom-call | tf_op jit(solution)/shard_map/attention/pallas_call | solution.py:78
  159.6 0.0 copy-start.2
  159.6 0.0 copy-start.3
  159.6 4.7 %all-to-all-start.1 = ((bf16[16,128,256]{2,1,0:T(8,128)(2,1)}), bf16[16,128,256]{2,1,0:T(8,128)(2,1)S(1)}, u32[]{:S(2)}, u32[]{:S(2)}) async-start(bf16[16,128,256]{2,1,0:T(8,128)(2,1)} %attention.1), calls=%async_computation.1 | async-start | bytes 2097152 | tf_op jit(solution)/shard_map/all_to_all | solution.py:132
  164.4 0.0 copy-done.1
  164.4 0.1 copy.9
  164.5 34.0 %all_gather.3.weight_ref = bf16[4096,64]{1,0:T(8,128)(2,1)} all-gather(bf16[256,64]{1,0:T(8,128)(2,1)S(1)} %copy.9), channel_id=1, replica_groups=mesh['comp'=32,'seq'=16] {'seq'}, dimensions={0}, use_global_device_ids=true | all-gather | bytes 557056 | tf_op jit(solution)/shard_map/all_gather | solution.py:130
  198.5 0.0 all-to-all-done.1.in_ref
  198.5 0.0 copy-start
  198.5 1.0 copy-done
  199.4 2.8 %project.1 = (bf16[128,4096]{1,0:T(8,128)(2,1)}, f32[32,8,128]{2,1,0:T(8,128)}) custom-call(bf16[16,128,256]{2,1,0:T(8,128)(2,1)} %copy-done, bf16[4096,64]{1,0:T(8,128)(2,1)} %all_gather.3.weight_ref), custom_call_target="tpu_custom_call" | custom-call | tf_op jit(solution)/shard_map/project/pallas_call | solution.py:111
  202.2 21.8 %all_to_all.16 = f32[32,8,128]{2,1,0:T(8,128)S(1)} all-to-all(f32[32,8,128]{2,1,0:T(8,128)} %get-tuple-element.6), channel_id=1, replica_groups=mesh['comp'=32,'seq'=16] {'comp'}, dimensions={0} | all-to-all | bytes 262144 | tf_op jit(solution)/shard_map/all_to_all | solution.py:134
  224.0 0.0 copy-done.2
  224.0 0.0 copy-done.3
  224.0 0.6 broadcast_multiply_fusion
Async XLA Ops:
  146.6 17.8 %copy-start.1 = (bf16[256,64]{0,1:T(8,128)(2,1)S(1)}, bf16[256,64]{0,1:T(8,128)(2,1)}, u32[]{:S(2)}) copy-start(bf16[256,64]{0,1:T(8,128)(2,1)} %param.11) | copy-start | bytes 98308
  159.6 64.4 %copy-start.2 = (f32[2,128]{1,0:T(2,128)S(1)}, f32[2,128]{1,0:T(2,128)}, u32[]{:S(2)}) copy-start(f32[2,128]{1,0:T(2,128)} %param.9) | copy-start | bytes 3076
  159.6 64.4 %copy-start.3 = (f32[2,128]{1,0:T(2,128)S(1)}, f32[2,128]{1,0:T(2,128)}, u32[]{:S(2)}) copy-start(f32[2,128]{1,0:T(2,128)} %param.10) | copy-start | bytes 3076
  159.6 38.8 %all-to-all-start.1 = ((bf16[16,128,256]{2,1,0:T(8,128)(2,1)}), bf16[16,128,256]{2,1,0:T(8,128)(2,1)S(1)}, u32[]{:S(2)}, u32[]{:S(2)}) async-start(bf16[16,128,256]{2,1,0:T(8,128)(2,1)} %attention.1), calls=%async_computation.1 | async-start | bytes 2097152 | tf_op jit(solution)/shard_map/all_to_all | solution.py:132
  198.5 1.0 copy-start

commit v2 on v1

v2 whole, which is shorter than its diff:
```python
import math

import jax
import jax.numpy as jnp
from jax import lax
from jax.experimental import pallas as pl
from jax.experimental.pallas import tpu as pltpu
from jax.sharding import PartitionSpec as P

HD = 128
BLOCK = 256

alpha_now = 0.6
sigma_now = 0.8
alpha_next = 0.8
sigma_next = 0.6
step_before = 0.4

VMEM = pl.BlockSpec(memory_space=pltpu.VMEM)
PARAMS = pltpu.CompilerParams(vmem_limit_bytes=16 * 1024 * 1024)


def pack(queries, keys, values, seq_count):
    tokens, width = queries.shape
    cols = width // seq_count
    each = 4

    def kernel(q_ref, k_ref, v_ref, out_ref, held, in_sem, out_sem):
        incoming = [
            [
                pltpu.make_async_copy(ref.at[:, pl.ds(d * cols, cols)], held.at[d, n], in_sem.at[n, d])
                for n, ref in enumerate((q_ref, k_ref, v_ref))
            ]
            for d in range(seq_count)
        ]
        outgoing = [
            pltpu.make_async_copy(held.at[pl.ds(d, each)], out_ref.at[pl.ds(d, each)], out_sem.at[d // each])
            for d in range(0, seq_count, each)
        ]
        for copies in incoming:
            for copy in copies:
                copy.start()
        for d, copies in enumerate(incoming):
            for copy in copies:
                copy.wait()
            if d % each == each - 1:
                outgoing[d // each].start()
        for copy in outgoing:
            copy.wait()

    return pl.pallas_call(
        kernel,
        out_shape=jax.ShapeDtypeStruct((seq_count, 3, tokens, cols), queries.dtype),
        in_specs=[pl.BlockSpec(memory_space=pltpu.HBM)] * 3,
        out_specs=pl.BlockSpec(memory_space=pltpu.HBM),
        scratch_shapes=[
            pltpu.VMEM((seq_count, 3, tokens, cols), queries.dtype),
            pltpu.SemaphoreType.DMA((3, seq_count)),
            pltpu.SemaphoreType.DMA((seq_count // each,)),
        ],
        compiler_params=pltpu.CompilerParams(vmem_limit_bytes=60 * 1024 * 1024),
        name="pack",
    )(queries, keys, values)


def attention(blocks, weight):
    seq_count, _, tokens, cols = blocks.shape
    channels = weight.shape[1]
    length = seq_count * tokens
    heads = cols // HD
    group = BLOCK // tokens
    fold = cols // channels
    rows = tokens // fold

    def kernel(in_ref, weight_ref, out_ref, value_wide):
        for h in range(heads):
            value_wide[h, :, :HD] = in_ref[:, 2, :, h * HD : (h + 1) * HD].reshape(length, HD)
            value_wide[h, :, HD:] = jnp.ones((length, HD), jnp.bfloat16)
        scale = HD ** (-0.5) * math.log2(math.e)
        for h in range(heads):
            head = slice(h * HD, (h + 1) * HD)
            for b in range(0, seq_count, group):
                scores = lax.dot_general(
                    in_ref[b : b + group, 0, :, head].reshape(BLOCK, HD),
                    in_ref[:, 1, :, head].reshape(length, HD),
                    (((1,), (1,)), ((), ())),
                    preferred_element_type=jnp.float32,
                )
                highest = jnp.max(scores, axis=1, keepdims=True)
                weights = jnp.exp2((scores - highest) * scale).astype(jnp.bfloat16)
                sums = jnp.dot(weights, value_wide[h], preferred_element_type=jnp.float32)
                result = (sums[:, :HD] / sums[:, HD:]).astype(jnp.bfloat16)
                for t in range(group):
                    out_ref[b + t, :tokens, head] = result[t * tokens : (t + 1) * tokens]
        for b in range(seq_count):
            partial = jnp.dot(out_ref[b, :tokens], weight_ref[...], preferred_element_type=jnp.float32)
            partial = partial.astype(jnp.bfloat16)
            for f in range(fold):
                out_ref[b, tokens:, f * channels : (f + 1) * channels] = partial[f * rows : (f + 1) * rows]

    return pl.pallas_call(
        kernel,
        out_shape=jax.ShapeDtypeStruct((seq_count, tokens + rows, cols), jnp.bfloat16),
        in_specs=[VMEM, VMEM],
        out_specs=VMEM,
        scratch_shapes=[pltpu.VMEM((heads, length, 2 * HD), jnp.bfloat16)],
        compiler_params=pltpu.CompilerParams(vmem_limit_bytes=32 * 1024 * 1024),
        name="attention",
    )(blocks, weight)


def noise_rows(returned, tokens, comp_count):
    seq_count, total_rows, cols = returned.shape
    rows = total_rows - tokens
    channels = cols * rows // tokens
    fold = cols // channels
    own = channels // comp_count
    width = seq_count * cols

    def kernel(in_ref, noise_ref):
        squares = jnp.zeros((tokens, cols), jnp.float32)
        total = jnp.zeros((rows, cols), jnp.float32)
        for d in range(seq_count):
            squares += jnp.square(in_ref[d, :tokens].astype(jnp.float32))
            total += in_ref[d, tokens:].astype(jnp.float32)
        root = jnp.sqrt(jnp.sum(squares, axis=1, keepdims=True) / width + 1e-06)
        projected = jnp.concatenate([total[:, f * channels : (f + 1) * channels] for f in range(fold)], axis=0)
        noise = jnp.concatenate([projected / root] * (tokens // channels), axis=1).T
        noise_ref[...] = jnp.zeros(noise_ref.shape, jnp.float32)
        for c in range(comp_count):
            noise_ref[c, :own, :] = noise[c * own : (c + 1) * own, :]

    return pl.pallas_call(
        kernel,
        out_shape=jax.ShapeDtypeStruct((comp_count, 8, tokens), jnp.float32),
        in_specs=[VMEM],
        out_specs=VMEM,
        compiler_params=PARAMS,
        name="noise",
    )(returned)


def assemble(returned, tokens):
    seq_count, _, cols = returned.shape

    def kernel(in_ref, out_ref):
        for d in range(seq_count):
            out_ref[:, d * cols : (d + 1) * cols] = in_ref[d, :tokens]

    return pl.pallas_call(
        kernel,
        out_shape=jax.ShapeDtypeStruct((tokens, seq_count * cols), jnp.bfloat16),
        in_specs=[VMEM],
        out_specs=VMEM,
        compiler_params=PARAMS,
        name="assemble",
    )(returned)


def on_device(queries, keys, values, latent, prev_denoised, head_weight):
    seq_count = lax.axis_size("seq")
    comp_count = lax.axis_size("comp")
    own_channels = latent.shape[0]
    tokens = queries.shape[1]
    packed = pack(queries[0], keys[0], values[0], seq_count)
    blocks = lax.all_to_all(packed, "seq", split_axis=0, concat_axis=0, tiled=True)
    outputs = attention(blocks, head_weight)
    returned = lax.all_to_all(outputs, "seq", split_axis=0, concat_axis=0, tiled=True)
    noise = noise_rows(returned, tokens, comp_count)
    everyone = lax.all_to_all(noise, "comp", split_axis=0, concat_axis=0, tiled=True)
    hidden = assemble(returned, tokens)
    noise_own = everyone[comp_count - 1, :own_channels]
    denoised = (latent - sigma_now * noise_own) / alpha_now
    step_now = math.log(alpha_next / sigma_next) - math.log(alpha_now / sigma_now)
    ratio = step_before / step_now
    blend = (1.0 + 0.5 / ratio) * denoised - 0.5 / ratio * prev_denoised
    new_latent = sigma_next / sigma_now * latent - alpha_next * (math.exp(-step_now) - 1.0) * blend
    return (hidden[None], new_latent, denoised)


def solution(mesh):
    return jax.shard_map(
        on_device,
        mesh=mesh,
        in_specs=(
            P("comp", "seq", None),
            P("comp", "seq", None),
            P("comp", "seq", None),
            P("comp", "seq"),
            P("comp", "seq"),
            P("seq", None),
        ),
        out_specs=(P("comp", "seq", None), P("comp", "seq"), P("comp", "seq")),
        check_vma=False,
    )
```

time: 225 us -> 110 us (0.49)
  the two profiles are of different devices: /device:TPU:1 before, /device:TPU:8 now
where the time goes in v2:
time: 110 us
  waiting for transfers between devices  49.4 us (45%)
  blocking collectives  22.4 us (20%)
  starting transfers between devices  20.8 us (19%)
  Pallas kernels  15.9 us (14%)
    all_to_all x1, waiting for transfers between devices, on_device(): lax.all_to_all(packed, 'seq', split_axis=0, concat_axis=0, tiled=True)  37.8 us
    all_to_all x1, blocking collectives, on_device(): lax.all_to_all(outputs, 'seq', split_axis=0, concat_axis=0, tiled=True)  22.4 us
    all_to_all x1, waiting for transfers between devices, on_device(): lax.all_to_all(noise, 'comp', split_axis=0, concat_axis=0, tiled=True)  11.6 us
    all_to_all x1, starting transfers between devices, on_device(): lax.all_to_all(noise, 'comp', split_axis=0, concat_axis=0, tiled=True)  11.4 us
    pallas_call x1, Pallas kernels, attention(): pl.pallas_call(kernel, out_shape=jax.ShapeDtypeStruct((seq_count, tokens...  10.5 us
    all_to_all x1, starting transfers between devices, on_device(): lax.all_to_all(packed, 'seq', split_axis=0, concat_axis=0, tiled=True)  9.37 us
    pallas_call x1, Pallas kernels, pack(): pl.pallas_call(kernel, out_shape=jax.ShapeDtypeStruct((seq_count, 3, toke...  3.29 us
  transfers between devices with their start and end apart: 2, of which 2 were waited for; matrix products, arithmetic and copies ran while one was open for 0% of the time, Pallas kernels for 1%

profile of v2, /device:TPU:8, one launch (start us, length us, event | category | flops | bytes accessed | tf_op | source)
XLA Modules:
  0.0 109.9 jit_solution(6657596416191120112)
XLA Ops:
  0.6 3.3 %pack.1 = bf16[16,3,128,256]{3,2,1,0:T(8,128)(2,1)} custom-call(bf16[128,4096]{1,0:T(8,128)(2,1)} %bitcast.13, bf16[128,4096]{1,0:T(8,128)(2,1)} %bitcast.14, bf16[128,4096]{1,0:T(8,128)(2,1)} %bitcast.15), custom_call_target="tpu_custom_call" | custom-call | tf_op jit(solution)/shard_map/pack/pallas_call | solution.py:51
  3.9 0.0 copy-start
  3.9 9.4 %all-to-all-start = ((bf16[16,3,128,256]{3,2,1,0:T(8,128)(2,1)}), bf16[16,3,128,256]{3,2,1,0:T(8,128)(2,1)S(1)}, u32[]{:S(2)}, u32[]{:S(2)}) async-start(bf16[16,3,128,256]{3,2,1,0:T(8,128)(2,1)} %pack.1), calls=%async_computation | async-start | bytes 6291456 | tf_op jit(solution)/shard_map/all_to_all | solution.py:166
  13.3 0.0 copy-done
  13.3 0.1 copy.9.weight_ref
  13.4 37.8 %all-to-all-done.in_ref = bf16[16,3,128,256]{3,2,1,0:T(8,128)(2,1)S(1)} async-done(((bf16[16,3,128,256]{3,2,1,0:T(8,128)(2,1)}), bf16[16,3,128,256]{3,2,1,0:T(8,128)(2,1)S(1)}, u32[]{:S(2)}, u32[]{:S(2)}) %all-to-all-start) | async-done | bytes 3145760 | tf_op jit(solution)/shard_map/all_to_all | solution.py:166
  51.2 10.5 %attention.1 = bf16[16,160,256]{2,1,0:T(8,128)(2,1)S(1)} custom-call(bf16[16,3,128,256]{3,2,1,0:T(8,128)(2,1)S(1)} %all-to-all-done.in_ref, bf16[256,64]{1,0:T(8,128)(2,1)S(1)} %copy.9.weight_ref), custom_call_target="tpu_custom_call" | custom-call | tf_op jit(solution)/shard_map/attention/pallas_call | solution.py:101
  61.7 0.0 copy-start.1
  61.7 0.0 copy-start.2
  61.7 22.4 %all_to_all.15.in_ref = bf16[16,160,256]{2,1,0:T(8,128)(2,1)S(1)} all-to-all(bf16[16,160,256]{2,1,0:T(8,128)(2,1)S(1)} %attention.1), channel_id=1, replica_groups=mesh['comp'=32,'seq'=16] {'seq'}, dimensions={0} | all-to-all | bytes 2621440 | tf_op jit(solution)/shard_map/all_to_all | solution.py:168
  84.1 1.1 noise.1
  85.2 11.4 %all-to-all-start.2 = ((f32[32,8,128]{2,1,0:T(8,128)}), f32[32,8,128]{2,1,0:T(8,128)S(1)}, u32[]{:S(2)}, u32[]{:S(2)}) async-start(f32[32,8,128]{2,1,0:T(8,128)} %noise.1), calls=%async_computation.2 | async-start | bytes 262144 | tf_op jit(solution)/shard_map/all_to_all | solution.py:170
  96.7 1.1 assemble.1
  97.7 11.6 %all-to-all-done.2 = f32[32,8,128]{2,1,0:T(8,128)S(1)} async-done(((f32[32,8,128]{2,1,0:T(8,128)}), f32[32,8,128]{2,1,0:T(8,128)S(1)}, u32[]{:S(2)}, u32[]{:S(2)}) %all-to-all-start.2) | async-done | bytes 131104 | tf_op jit(solution)/shard_map/all_to_all | solution.py:170
  109.3 0.0 copy-done.1
  109.3 0.0 copy-done.2
  109.3 0.6 broadcast_multiply_fusion
Async XLA Ops:
  3.9 9.4 %copy-start = (bf16[256,64]{0,1:T(8,128)(2,1)S(1)}, bf16[256,64]{0,1:T(8,128)(2,1)}, u32[]{:S(2)}) copy-start(bf16[256,64]{0,1:T(8,128)(2,1)} %param.11) | copy-start | bytes 98308
  3.9 47.3 %all-to-all-start = ((bf16[16,3,128,256]{3,2,1,0:T(8,128)(2,1)}), bf16[16,3,128,256]{3,2,1,0:T(8,128)(2,1)S(1)}, u32[]{:S(2)}, u32[]{:S(2)}) async-start(bf16[16,3,128,256]{3,2,1,0:T(8,128)(2,1)} %pack.1), calls=%async_computation | async-start | bytes 6291456 | tf_op jit(solution)/shard_map/all_to_all | solution.py:166
  61.7 47.7 %copy-start.1 = (f32[2,128]{1,0:T(2,128)S(1)}, f32[2,128]{1,0:T(2,128)}, u32[]{:S(2)}) copy-start(f32[2,128]{1,0:T(2,128)} %param.9) | copy-start | bytes 3076
  61.7 47.7 %copy-start.2 = (f32[2,128]{1,0:T(2,128)S(1)}, f32[2,128]{1,0:T(2,128)}, u32[]{:S(2)}) copy-start(f32[2,128]{1,0:T(2,128)} %param.10) | copy-start | bytes 3076
  85.2 24.1 %all-to-all-start.2 = ((f32[32,8,128]{2,1,0:T(8,128)}), f32[32,8,128]{2,1,0:T(8,128)S(1)}, u32[]{:S(2)}, u32[]{:S(2)}) async-start(f32[32,8,128]{2,1,0:T(8,128)} %noise.1), calls=%async_computation.2 | async-start | bytes 262144 | tf_op jit(solution)/shard_map/all_to_all | solution.py:170

commit v3 on v2

--- a/solution.py
+++ b/solution.py
@@ -23,49 +23,32 @@
 def pack(queries, keys, values, seq_count):
     tokens, width = queries.shape
     cols = width // seq_count
-    each = 4
 
-    def kernel(q_ref, k_ref, v_ref, out_ref, held, in_sem, out_sem):
-        incoming = [
-            [
-                pltpu.make_async_copy(ref.at[:, pl.ds(d * cols, cols)], held.at[d, n], in_sem.at[n, d])
-                for n, ref in enumerate((q_ref, k_ref, v_ref))
-            ]
+    def kernel(q_ref, k_ref, v_ref, out_ref, sem):
+        copies = [
+            pltpu.make_async_copy(ref.at[:, pl.ds(d * cols, cols)], out_ref.at[d, n], sem.at[n, d])
+            for n, ref in enumerate((q_ref, k_ref, v_ref))
             for d in range(seq_count)
         ]
-        outgoing = [
-            pltpu.make_async_copy(held.at[pl.ds(d, each)], out_ref.at[pl.ds(d, each)], out_sem.at[d // each])
-            for d in range(0, seq_count, each)
-        ]
-        for copies in incoming:
-            for copy in copies:
-                copy.start()
-        for d, copies in enumerate(incoming):
-            for copy in copies:
-                copy.wait()
-            if d % each == each - 1:
-                outgoing[d // each].start()
-        for copy in outgoing:
+        for copy in copies:
+            copy.start()
+        for copy in copies:
             copy.wait()
 
     return pl.pallas_call(
         kernel,
         out_shape=jax.ShapeDtypeStruct((seq_count, 3, tokens, cols), queries.dtype),
         in_specs=[pl.BlockSpec(memory_space=pltpu.HBM)] * 3,
-        out_specs=pl.BlockSpec(memory_space=pltpu.HBM),
-        scratch_shapes=[
-            pltpu.VMEM((seq_count, 3, tokens, cols), queries.dtype),
-            pltpu.SemaphoreType.DMA((3, seq_count)),
-            pltpu.SemaphoreType.DMA((seq_count // each,)),
-        ],
-        compiler_params=pltpu.CompilerParams(vmem_limit_bytes=60 * 1024 * 1024),
+        out_specs=VMEM,
+        scratch_shapes=[pltpu.SemaphoreType.DMA((3, seq_count))],
+        compiler_params=pltpu.CompilerParams(vmem_limit_bytes=16 * 1024 * 1024),
         name="pack",
     )(queries, keys, values)
 
 
 def attention(blocks, weight):
     seq_count, _, tokens, cols = blocks.shape
-    channels = weight.shape[1]
+    channels = weight.shape[0]
     length = seq_count * tokens
     heads = cols // HD
     group = BLOCK // tokens
@@ -92,11 +75,18 @@
                 result = (sums[:, :HD] / sums[:, HD:]).astype(jnp.bfloat16)
                 for t in range(group):
                     out_ref[b + t, :tokens, head] = result[t * tokens : (t + 1) * tokens]
-        for b in range(seq_count):
-            partial = jnp.dot(out_ref[b, :tokens], weight_ref[...], preferred_element_type=jnp.float32)
-            partial = partial.astype(jnp.bfloat16)
-            for f in range(fold):
-                out_ref[b, tokens:, f * channels : (f + 1) * channels] = partial[f * rows : (f + 1) * rows]
+
+        @pl.when(lax.axis_index("comp") == lax.axis_size("comp") - 1)
+        def _():
+            for b in range(seq_count):
+                partial = lax.dot_general(
+                    out_ref[b, :tokens],
+                    weight_ref[...],
+                    (((1,), (1,)), ((), ())),
+                    preferred_element_type=jnp.float32,
+                ).astype(jnp.bfloat16)
+                for f in range(fold):
+                    out_ref[b, tokens:, f * channels : (f + 1) * channels] = partial[f * rows : (f + 1) * rows]
 
     return pl.pallas_call(
         kernel,
@@ -118,21 +108,22 @@
     width = seq_count * cols
 
     def kernel(in_ref, noise_ref):
-        squares = jnp.zeros((tokens, cols), jnp.float32)
-        total = jnp.zeros((rows, cols), jnp.float32)
-        for d in range(seq_count):
-            squares += jnp.square(in_ref[d, :tokens].astype(jnp.float32))
-            total += in_ref[d, tokens:].astype(jnp.float32)
-        root = jnp.sqrt(jnp.sum(squares, axis=1, keepdims=True) / width + 1e-06)
-        projected = jnp.concatenate([total[:, f * channels : (f + 1) * channels] for f in range(fold)], axis=0)
-        noise = jnp.concatenate([projected / root] * (tokens // channels), axis=1).T
-        noise_ref[...] = jnp.zeros(noise_ref.shape, jnp.float32)
-        for c in range(comp_count):
-            noise_ref[c, :own, :] = noise[c * own : (c + 1) * own, :]
+        @pl.when(lax.axis_index("comp") == comp_count - 1)
+        def _():
+            squares = jnp.zeros((tokens, cols), jnp.float32)
+            total = jnp.zeros((rows, cols), jnp.float32)
+            for d in range(seq_count):
+                squares += jnp.square(in_ref[d, :tokens].astype(jnp.float32))
+                total += in_ref[d, tokens:].astype(jnp.float32)
+            root = jnp.sqrt(jnp.sum(squares, axis=1, keepdims=True) / width + 1e-06)
+            projected = jnp.concatenate([total[:, f * channels : (f + 1) * channels] for f in range(fold)], axis=0)
+            noise = jnp.concatenate([projected / root] * (tokens // channels), axis=1).T
+            for c in range(comp_count):
+                noise_ref[c] = noise[c * own : (c + 1) * own, :]
 
     return pl.pallas_call(
         kernel,
-        out_shape=jax.ShapeDtypeStruct((comp_count, 8, tokens), jnp.float32),
+        out_shape=jax.ShapeDtypeStruct((comp_count, own, tokens), jnp.float32),
         in_specs=[VMEM],
         out_specs=VMEM,
         compiler_params=PARAMS,
@@ -160,16 +151,15 @@
 def on_device(queries, keys, values, latent, prev_denoised, head_weight):
     seq_count = lax.axis_size("seq")
     comp_count = lax.axis_size("comp")
-    own_channels = latent.shape[0]
     tokens = queries.shape[1]
-    packed = pack(queries[0], keys[0], values[0], seq_count)
+    packed = pack(*(pltpu.with_memory_space_constraint(x[0], pltpu.HBM) for x in (queries, keys, values)), seq_count)
     blocks = lax.all_to_all(packed, "seq", split_axis=0, concat_axis=0, tiled=True)
-    outputs = attention(blocks, head_weight)
+    outputs = attention(blocks, head_weight.T)
     returned = lax.all_to_all(outputs, "seq", split_axis=0, concat_axis=0, tiled=True)
     noise = noise_rows(returned, tokens, comp_count)
     everyone = lax.all_to_all(noise, "comp", split_axis=0, concat_axis=0, tiled=True)
     hidden = assemble(returned, tokens)
-    noise_own = everyone[comp_count - 1, :own_channels]
+    noise_own = everyone[comp_count - 1]
     denoised = (latent - sigma_now * noise_own) / alpha_now
     step_now = math.log(alpha_next / sigma_next) - math.log(alpha_now / sigma_now)
     ratio = step_before / step_now

time: 110 us -> 107 us (0.973)
  blocking collectives: 22.4 us -> 68.1 us
  waiting for transfers between devices: 49.4 us -> 11.1 us
  starting transfers between devices: 20.8 us -> 12.3 us
  Pallas kernels: 15.9 us -> 14.4 us
    all_to_all x0 -> x1, blocking collectives: none -> 46.2 us  [on_device(): lax.all_to_all(packed, 'seq', split_axis=0, concat_axis=0, tiled=True)]
    all_to_all x1 -> x0, waiting for transfers between devices: 37.8 us -> none  [on_device(): lax.all_to_all(packed, 'seq', split_axis=0, concat_axis=0, tiled=True)]
    all_to_all x1 -> x0, starting transfers between devices: 9.37 us -> none  [on_device(): lax.all_to_all(packed, 'seq', split_axis=0, concat_axis=0, tiled=True)]
  transfers between devices with their start and end apart: 2 -> 1, of which waited for: 2 -> 1; matrix products, arithmetic and copies ran while one was open for 0% -> 0% of each run, Pallas kernels for 1% -> 1%
where the time goes in v3:
time: 107 us
  blocking collectives  68.1 us (64%)
  Pallas kernels  14.4 us (13%)
  starting transfers between devices  12.3 us (11%)
  waiting for transfers between devices  11.1 us (10%)
    all_to_all x1, blocking collectives, on_device(): lax.all_to_all(packed, 'seq', split_axis=0, concat_axis=0, tiled=True)  46.2 us
    all_to_all x1, blocking collectives, on_device(): lax.all_to_all(outputs, 'seq', split_axis=0, concat_axis=0, tiled=True)  21.9 us
    all_to_all x1, starting transfers between devices, on_device(): lax.all_to_all(noise, 'comp', split_axis=0, concat_axis=0, tiled=True)  12.3 us
    all_to_all x1, waiting for transfers between devices, on_device(): lax.all_to_all(noise, 'comp', split_axis=0, concat_axis=0, tiled=True)  11.1 us
    pallas_call x1, Pallas kernels, attention(): pl.pallas_call(kernel, out_shape=jax.ShapeDtypeStruct((seq_count, tokens...  10.3 us
    pallas_call x1, Pallas kernels, pack(): pl.pallas_call(kernel, out_shape=jax.ShapeDtypeStruct((seq_count, 3, toke...  2.34 us
  transfers between devices with their start and end apart: 1, of which 1 were waited for; matrix products, arithmetic and copies ran while one was open for 0% of the time, Pallas kernels for 1%

profile of v3, /device:TPU:8, one launch (start us, length us, event | category | flops | bytes accessed | tf_op | source)
XLA Modules:
  0.0 107.1 jit_solution(14435459277504738820)
XLA Ops:
  0.6 2.3 %pack.1 = bf16[16,3,128,256]{3,2,1,0:T(8,128)(2,1)S(1)} custom-call(bf16[128,4096]{1,0:T(8,128)(2,1)} %bitcast.15, bf16[128,4096]{1,0:T(8,128)(2,1)} %bitcast.16, bf16[128,4096]{1,0:T(8,128)(2,1)} %bitcast.17), custom_call_target="tpu_custom_call" | custom-call | tf_op jit(solution)/shard_map/pack/pallas_call | solution.py:38
  3.0 0.0 copy-start
  3.0 46.2 %all_to_all.15.in_ref = bf16[16,3,128,256]{3,2,1,0:T(8,128)(2,1)S(1)} all-to-all(bf16[16,3,128,256]{3,2,1,0:T(8,128)(2,1)S(1)} %pack.1), channel_id=1, replica_groups=mesh['comp'=32,'seq'=16] {'seq'}, dimensions={0} | all-to-all | bytes 6291456 | tf_op jit(solution)/shard_map/all_to_all | solution.py:156
  49.2 0.0 copy-done
  49.2 10.3 %attention.1 = bf16[16,160,256]{2,1,0:T(8,128)(2,1)S(1)} custom-call(bf16[16,3,128,256]{3,2,1,0:T(8,128)(2,1)S(1)} %all_to_all.15.in_ref, bf16[64,256]{1,0:T(8,128)(2,1)S(1)} %bitcast.13), custom_call_target="tpu_custom_call" | custom-call | tf_op jit(solution)/shard_map/attention/pallas_call | solution.py:91
  59.5 0.0 copy-start.1
  59.5 0.0 copy-start.2
  59.5 21.9 %all_to_all.16.in_ref = bf16[16,160,256]{2,1,0:T(8,128)(2,1)S(1)} all-to-all(bf16[16,160,256]{2,1,0:T(8,128)(2,1)S(1)} %attention.1), channel_id=1, replica_groups=mesh['comp'=32,'seq'=16] {'seq'}, dimensions={0} | all-to-all | bytes 2621440 | tf_op jit(solution)/shard_map/all_to_all | solution.py:158
  81.4 0.6 noise.1
  82.0 12.3 %all-to-all-start.2 = ((f32[32,2,128]{2,1,0:T(2,128)}), f32[32,2,128]{2,1,0:T(2,128)S(1)}, u32[]{:S(2)}, u32[]{:S(2)}) async-start(f32[32,2,128]{2,1,0:T(2,128)} %noise.1), calls=%async_computation.2 | async-start | bytes 65536 | tf_op jit(solution)/shard_map/all_to_all | solution.py:160
  94.3 1.1 %assemble.1 = bf16[128,4096]{1,0:T(8,128)(2,1)} custom-call(bf16[16,160,256]{2,1,0:T(8,128)(2,1)S(1)} %all_to_all.16.in_ref), custom_call_target="tpu_custom_call" | custom-call | tf_op jit(solution)/shard_map/assemble/pallas_call | solution.py:141
  95.4 11.1 %all-to-all-done.2 = f32[32,2,128]{2,1,0:T(2,128)S(1)} async-done(((f32[32,2,128]{2,1,0:T(2,128)}), f32[32,2,128]{2,1,0:T(2,128)S(1)}, u32[]{:S(2)}, u32[]{:S(2)}) %all-to-all-start.2) | async-done | bytes 32800 | tf_op jit(solution)/shard_map/all_to_all | solution.py:160
  106.5 0.0 copy-done.1
  106.5 0.0 copy-done.2
  106.5 0.6 broadcast_multiply_fusion
Async XLA Ops:
  3.0 46.2 %copy-start = (bf16[256,64]{0,1:T(8,128)(2,1)S(1)}, bf16[256,64]{0,1:T(8,128)(2,1)}, u32[]{:S(2)}) copy-start(bf16[256,64]{0,1:T(8,128)(2,1)} %param.11) | copy-start | bytes 98308
  59.5 47.0 %copy-start.1 = (f32[2,128]{1,0:T(2,128)S(1)}, f32[2,128]{1,0:T(2,128)}, u32[]{:S(2)}) copy-start(f32[2,128]{1,0:T(2,128)} %param.9) | copy-start | bytes 3076
  59.5 47.0 %copy-start.2 = (f32[2,128]{1,0:T(2,128)S(1)}, f32[2,128]{1,0:T(2,128)}, u32[]{:S(2)}) copy-start(f32[2,128]{1,0:T(2,128)} %param.10) | copy-start | bytes 3076
  82.0 24.5 %all-to-all-start.2 = ((f32[32,2,128]{2,1,0:T(2,128)}), f32[32,2,128]{2,1,0:T(2,128)S(1)}, u32[]{:S(2)}, u32[]{:S(2)}) async-start(f32[32,2,128]{2,1,0:T(2,128)} %noise.1), calls=%async_computation.2 | async-start | bytes 65536 | tf_op jit(solution)/shard_map/all_to_all | solution.py:160

commit v4 on v3

v4 whole, which is shorter than its diff:
```python
import math

import jax
import jax.numpy as jnp
from jax import lax
from jax.experimental import pallas as pl
from jax.experimental.pallas import tpu as pltpu
from jax.sharding import PartitionSpec as P

HD = 128
BLOCK = 256
NEAR = 8

alpha_now = 0.6
sigma_now = 0.8
alpha_next = 0.8
sigma_next = 0.6
step_before = 0.4

VMEM = pl.BlockSpec(memory_space=pltpu.VMEM)
PARAMS = pltpu.CompilerParams(vmem_limit_bytes=16 * 1024 * 1024)


def pack(queries, keys, values, seq_count):
    tokens, width = queries.shape
    cols = width // seq_count
    chunks = 2
    rows = tokens // chunks

    def kernel(q_ref, k_ref, v_ref, out_ref, held, sem):
        copies = [
            [
                pltpu.make_async_copy(ref.at[pl.ds(c * rows, rows)], held.at[n, pl.ds(c * rows, rows)], sem.at[n, c])
                for c in range(chunks)
            ]
            for n, ref in enumerate((q_ref, k_ref, v_ref))
        ]
        for n in range(3):
            for copy in copies[n]:
                copy.start()
        for n in range(3):
            for c, copy in enumerate(copies[n]):
                copy.wait()
                span = slice(c * rows, (c + 1) * rows)
                for d in range(seq_count):
                    out_ref[d, n, span] = held[n, span, d * cols : (d + 1) * cols]

    return pl.pallas_call(
        kernel,
        out_shape=jax.ShapeDtypeStruct((seq_count, 3, tokens, cols), queries.dtype),
        in_specs=[pl.BlockSpec(memory_space=pltpu.HBM)] * 3,
        out_specs=VMEM,
        scratch_shapes=[
            pltpu.VMEM((3, tokens, width), queries.dtype),
            pltpu.SemaphoreType.DMA((3, chunks)),
        ],
        compiler_params=PARAMS,
        name="pack",
    )(queries, keys, values)


def attention(blocks, weight, noise_shapes=None):
    seq_count, _, tokens, cols = blocks.shape
    channels = weight.shape[0]
    length = seq_count * tokens
    heads = cols // HD
    group = BLOCK // tokens
    project = noise_shapes is None
    others = [jax.ShapeDtypeStruct((seq_count, channels + 16, tokens), jnp.bfloat16)] if project else noise_shapes

    def kernel(in_ref, weight_ref, out_ref, *other_refs):
        scale = HD ** (-0.5) * math.log2(math.e)

        def scores_of(h, b):
            head = slice(h * HD, (h + 1) * HD)
            return lax.dot_general(
                in_ref[b : b + group, 0, :, head].reshape(BLOCK, HD),
                in_ref[:, 1, :, head].reshape(length, HD),
                (((1,), (1,)), ((), ())),
                preferred_element_type=jnp.float32,
            )

        steps = [(h, b) for h in range(heads) for b in range(0, seq_count, group)]
        upcoming = scores_of(*steps[0])
        for step, (h, b) in enumerate(steps):
            scores = upcoming
            if step + 1 < len(steps):
                upcoming = scores_of(*steps[step + 1])
            head = slice(h * HD, (h + 1) * HD)
            value = in_ref[:, 2, :, head].reshape(length, HD)
            highest = jnp.max(scores, axis=1, keepdims=True)
            weights = jnp.exp2((scores - highest) * scale).astype(jnp.bfloat16)
            sums = jnp.dot(
                weights,
                jnp.concatenate([value, jnp.ones((length, HD), jnp.bfloat16)], axis=1),
                preferred_element_type=jnp.float32,
            )
            result = (sums[:, :HD] / sums[:, HD:]).astype(jnp.bfloat16)
            for t in range(group):
                out_ref[b + t, :, head] = result[t * tokens : (t + 1) * tokens]

        for part_ref in other_refs if project else ():
            contract = (((1,), (1,)), ((), ()))
            ones = jnp.ones((8, cols), jnp.bfloat16)
            for b in range(seq_count):
                hidden = out_ref[b]
                partial = lax.dot_general(weight_ref[...], hidden, contract, preferred_element_type=jnp.float32)
                part_ref[b, :channels] = partial.astype(jnp.bfloat16)
                square = jnp.square(hidden.astype(jnp.float32))
                high = square.astype(jnp.bfloat16)
                low = (square - high.astype(jnp.float32)).astype(jnp.bfloat16)
                total = lax.dot_general(ones, high, contract, preferred_element_type=jnp.float32)
                total += lax.dot_general(ones, low, contract, preferred_element_type=jnp.float32)
                coarse = total.astype(jnp.bfloat16).astype(jnp.float32)
                part_ref[b, channels:] = jnp.concatenate([coarse, total - coarse], axis=0).astype(jnp.bfloat16)

    return pl.pallas_call(
        kernel,
        out_shape=[jax.ShapeDtypeStruct((seq_count, tokens, cols), jnp.bfloat16), *others],
        in_specs=[VMEM, VMEM],
        out_specs=[VMEM] * (1 + len(others)),
        compiler_params=pltpu.CompilerParams(vmem_limit_bytes=32 * 1024 * 1024),
        name="attention",
    )(blocks, weight)


def noise_shapes_of(comp_count, own, tokens):
    run = jax.ShapeDtypeStruct((NEAR, own, tokens), jnp.float32)
    return [run] * (comp_count // NEAR) + [jax.ShapeDtypeStruct((own, tokens), jnp.float32)]


def noise_parts(returned, width, noise_shapes):
    seq_count, total_rows, tokens = returned.shape
    channels = total_rows - 16
    own = noise_shapes[-1].shape[0]

    def kernel(in_ref, *out_refs):
        total = jnp.zeros((total_rows, tokens), jnp.float32)
        for d in range(seq_count):
            total += in_ref[d].astype(jnp.float32)
        squares = total[channels : channels + 1] + total[channels + 8 : channels + 9]
        noise = total[:channels] / jnp.sqrt(squares / width + 1e-06)
        for r, out_ref in enumerate(out_refs[:-1]):
            for n in range(NEAR):
                start = (r * NEAR + n) * own
                out_ref[n] = noise[start : start + own]
        out_refs[-1][...] = noise[channels - own :]

    return pl.pallas_call(
        kernel,
        out_shape=noise_shapes,
        in_specs=[VMEM],
        out_specs=[VMEM] * len(noise_shapes),
        compiler_params=PARAMS,
        name="noise",
    )(returned)


def assemble(returned):
    seq_count, tokens, cols = returned.shape

    def kernel(in_ref, out_ref):
        for d in range(seq_count):
            out_ref[:, d * cols : (d + 1) * cols] = in_ref[d]

    return pl.pallas_call(
        kernel,
        out_shape=jax.ShapeDtypeStruct((tokens, seq_count * cols), jnp.bfloat16),
        in_specs=[VMEM],
        out_specs=VMEM,
        compiler_params=PARAMS,
        name="assemble",
    )(returned)


def on_device(queries, keys, values, latent, prev_denoised, head_weight):
    seq_count = lax.axis_size("seq")
    comp_count = lax.axis_size("comp")
    tokens = queries.shape[1]
    last = comp_count - 1
    comp = lax.axis_index("comp")
    queries, keys, values, comp = lax.optimization_barrier((queries, keys, values, comp))
    packed = pack(*(pltpu.with_memory_space_constraint(x[0], pltpu.HBM) for x in (queries, keys, values)), seq_count)
    blocks = lax.all_to_all(packed, "seq", split_axis=0, concat_axis=0, tiled=True)
    own = latent.shape[0]
    width = queries.shape[2]
    noise_shapes = noise_shapes_of(comp_count, own, tokens)
    half = NEAR // 2
    runs = [list(range(first, first + NEAR)) for first in range(0, comp_count, NEAR)]

    def exchange(array):
        return lax.all_to_all(array, "seq", split_axis=0, concat_axis=0, tiled=True)

    def exchange_grouped(array):
        group = [list(range(seq_count))]
        return lax.all_to_all(array, "seq", split_axis=0, concat_axis=0, tiled=True, axis_index_groups=group)

    def on_last(blocks, weight):
        outputs, parts = attention(blocks, weight)
        return outputs, *noise_parts(exchange(parts), width, noise_shapes)

    def elsewhere(blocks, weight):
        return tuple(attention(blocks, weight, noise_shapes))

    blocks, comp = lax.optimization_barrier((blocks, comp))
    outputs, *noise = lax.cond(comp == last, on_last, elsewhere, blocks, head_weight.T)
    sent = [lax.ppermute(noise[r], "comp", [(last, run[half - 1])]) for r, run in enumerate(runs)]
    returned = lax.cond(comp == last, exchange, exchange_grouped, outputs)
    returned, sent = lax.optimization_barrier((returned, sent))
    hidden = assemble(returned)
    part = sum(sent[1:], sent[0])

    def own_of_last(part):
        return noise[-1]

    def from_holders(part):
        holders = [(run[half - 1], run[-1] if run[-1] != last else run[-2]) for run in runs]
        passed = lax.ppermute(part[half:], "comp", holders)
        held = jnp.where(comp % NEAR == half - 1, part[:half], passed)
        result = jnp.zeros((own, tokens), jnp.float32)
        for n in range(half):
            pairs = []
            for run, (first, second) in zip(runs, holders):
                pairs += [(first, run[n]), (second, run[half + n])]
            pairs = [(source, target) for source, target in pairs if target not in (source, last)]
            if pairs:
                result += lax.ppermute(held[n], "comp", pairs)
        kept = (comp % NEAR == half - 1) | (comp % NEAR == NEAR - 1)
        result = jnp.where(kept, held[half - 1], result)
        return jnp.where(comp == last - 1, held[half - 2], result)

    noise_own = lax.cond(comp == last, own_of_last, from_holders, part)
    denoised = (latent - sigma_now * noise_own) / alpha_now
    step_now = math.log(alpha_next / sigma_next) - math.log(alpha_now / sigma_now)
    ratio = step_before / step_now
    blend = (1.0 + 0.5 / ratio) * denoised - 0.5 / ratio * prev_denoised
    new_latent = sigma_next / sigma_now * latent - alpha_next * (math.exp(-step_now) - 1.0) * blend
    return (hidden[None], new_latent, denoised)


def solution(mesh):
    return jax.shard_map(
        on_device,
        mesh=mesh,
        in_specs=(
            P("comp", "seq", None),
            P("comp", "seq", None),
            P("comp", "seq", None),
            P("comp", "seq"),
            P("comp", "seq"),
            P("seq", None),
        ),
        out_specs=(P("comp", "seq", None), P("comp", "seq"), P("comp", "seq")),
        check_vma=False,
    )
```

time: 107 us -> 97 us (0.907)
  the two profiles are of different devices: /device:TPU:8 before, /device:TPU:448 now
where the time goes in v4:
time: 97 us; the launch traced here: 96.6 us
  blocking collectives  63.3 us (65%)
  waiting for transfers between devices  13 us (13%)
  Pallas kernels  12.7 us (13%)
  starting transfers between devices  5.91 us (6%)
    all_to_all x1, blocking collectives, on_device(): lax.all_to_all(packed, 'seq', split_axis=0, concat_axis=0, tiled=True)  44.2 us
    all_to_all x1, blocking collectives, exchange_grouped(): lax.all_to_all(array, 'seq', split_axis=0, concat_axis=0, tiled=True, axi...  19.1 us
    ppermute x3, waiting for transfers between devices, from_holders(): result += lax.ppermute(held[n], 'comp', pairs)  13 us
    pallas_call x1, Pallas kernels, attention(): pl.pallas_call(kernel, out_shape=[jax.ShapeDtypeStruct((seq_count, tokens...  9.74 us
    ppermute x4, starting transfers between devices, on_device(): lax.ppermute(noise[r], 'comp', [(last, run[half - 1])])  2.65 us
    ppermute x3, starting transfers between devices, from_holders(): result += lax.ppermute(held[n], 'comp', pairs)  2.62 us
  transfers between devices with their start and end apart: 8, of which 1 were waited for; matrix products, arithmetic and copies ran while one was open for 0% of the time, Pallas kernels for 0%

profile of v4, /device:TPU:448, one launch (start us, length us, event | category | flops | bytes accessed | tf_op | source)
XLA Modules:
  0.0 96.6 jit_solution(10756711716269137869)
XLA Ops:
  0.6 1.9 %pack.1 = bf16[16,3,128,256]{3,2,1,0:T(8,128)(2,1)S(1)} custom-call(bf16[128,4096]{1,0:T(8,128)(2,1)} %bitcast.25, bf16[128,4096]{1,0:T(8,128)(2,1)} %bitcast.26, bf16[128,4096]{1,0:T(8,128)(2,1)} %bitcast.27), custom_call_target="tpu_custom_call" | custom-call | tf_op jit(solution)/shard_map/pack/pallas_call | solution.py:48
  2.6 0.0 copy-start
  2.6 44.2 %all_to_all.20 = bf16[16,3,128,256]{3,2,1,0:T(8,128)(2,1)S(1)} all-to-all(bf16[16,3,128,256]{3,2,1,0:T(8,128)(2,1)S(1)} %pack.1), channel_id=1, replica_groups=mesh['comp'=32,'seq'=16] {'seq'}, dimensions={0} | all-to-all | bytes 6291456 | tf_op jit(solution)/shard_map/all_to_all | solution.py:184
  46.7 0.0 copy-done
  46.7 10.0 %conditional.3 = (f32[8,2,128]{2,1,0:T(2,128)S(1)}, f32[8,2,128]{2,1,0:T(2,128)S(1)}, f32[8,2,128]{2,1,0:T(2,128)S(1)}, f32[8,2,128]{2,1,0:T(2,128)S(1)}, bf16[1...) conditional(s32[]{:T(128)} %convert_element_type.2, (bf16[16,3,128,256]{3,2,1,0:T(8,128)(2,1)S(1)}, ...), branch_computations={%region_0.0_spmd, %region_1.0_spmd} | conditional | bytes 655408 | solution.py:206
  46.7 9.7 %attention.2 = (bf16[16,128,256]{2,1,0:T(8,128)(2,1)S(1)}, f32[8,2,128]{2,1,0:T(2,128)S(1)}, f32[8,2,128]{2,1,0:T(2,128)S(1)}, f32[8,2,128]{2,1,0:T(2,128)S(1)},...) custom-call(bf16[16,3,128,256]{3,2,1,0:T(8,128)(2,1)S(1)} %get-tuple-element.38.in_ref, ...), custom_call_target="tpu_custom_call" | custom-call | tf_op jit(solution)/shard_map/cond/branch_0_fun/attention/pallas_call | solution.py:117
  56.7 0.7 collective-permute-start.4
  57.4 0.7 collective-permute-start.5
  58.1 0.7 collective-permute-start.6
  58.7 0.7 collective-permute-start.7
  59.4 0.0 copy-start.1
  59.4 0.0 copy-start.2
  59.4 19.1 %conditional.4 = (bf16[16,128,256]{2,1,0:T(8,128)(2,1)S(1)}) conditional(s32[]{:T(128)} %convert_element_type.2, bf16[16,128,256]{2,1,0:T(8,128)(2,1)S(1)} %get-tuple-element.86, bf16[16,128,256]{2,1,0:T(8,128)(2,1)S(1)} %get-tuple-element.86), branch_computations={%region_2.0_spmd, %region_3.0_spmd} | conditional | bytes 2097160 | solution.py:208
  59.4 19.1 %all_to_all.18 = bf16[16,128,256]{2,1,0:T(8,128)(2,1)S(1)} all-to-all(bf16[16,128,256]{2,1,0:T(8,128)(2,1)S(1)} %param.2), channel_id=1, replica_groups={{0,1,2,3,4,5,6,7,8,9,10,11,12,13,14,15},{16,17,18,19,20,21,22,23,24,25,..., dimensions={0} | all-to-all | bytes 2097152 | tf_op jit(solution)/shard_map/cond/branch_0_fun/all_to_all | solution.py:196
  78.5 0.0 collective-permute-done.4
  78.6 0.0 collective-permute-done.5
  78.6 0.0 collective-permute-done.6
  78.6 0.0 collective-permute-done.7
  78.6 1.1 %assemble.1 = bf16[128,4096]{1,0:T(8,128)(2,1)} custom-call(bf16[16,128,256]{2,1,0:T(8,128)(2,1)S(1)} %get-tuple-element.114.in_ref), custom_call_target="tpu_custom_call" | custom-call | tf_op jit(solution)/shard_map/assemble/pallas_call | solution.py:166
  79.6 16.4 %conditional.5 = (f32[2,128]{1,0:T(2,128)S(1)}) conditional(s32[]{:T(128)} %convert_element_type.2, (s32[]{:T(128)}, f32[8,2,128]{2,1,0:T(2,128)S(1)}, f32[8,2,128]{2,1,0:T(2,128)S(1)}, f32[8,2,128]{2,1,0:T(2,128)S(1)}, f32[8,2,128]{2,1,0:T(2,128)S(1)}) %tuple.43, f32[2,128]{1,0:T(2,128)S(1)} %get-tuple-element.96), branch_computations={%region_4.5_spmd, %region_5.6_spmd} | conditional | flops 8207 | bytes 102710 | solution.py:232
  79.7 0.6 collective-permute-start
  80.3 0.0 collective-permute-done
  80.4 0.7 collective-permute-start.2
  81.0 1.3 %collective-permute-start.1 = (f32[2,128]{1,0:T(2,128)S(1)}, f32[2,128]{1,0:T(2,128)S(1)}, u32[]{:S(2)}, u32[]{:S(2)}) collective-permute-start(f32[2,128]{1,0:T(2,128)S(1)} %get-tuple-element.98), channel_id=1, source_target_pairs={{48,0},{112,64},{176,128},{240,192},{304,256},{368,320},{432,384},... | collective-permute-start | bytes 3080 | tf_op jit(solution)/shard_map/cond/branch_0_fun/ppermute | solution.py:227
  82.3 0.7 collective-permute-start.3
  83.0 0.0 collective-permute-done.2
  83.0 13.0 %collective-permute-done.1 = f32[2,128]{1,0:T(2,128)S(1)} collective-permute-done((f32[2,128]{1,0:T(2,128)S(1)}, f32[2,128]{1,0:T(2,128)S(1)}, u32[]{:S(2)}, u32[]{:S(2)}) %collective-permute-start.1) | collective-permute-done | bytes 1056 | tf_op jit(solution)/shard_map/cond/branch_0_fun/ppermute | solution.py:227
  96.0 0.0 collective-permute-done.3
  96.0 0.0 copy-done.1
  96.0 0.0 copy-done.2
  96.0 0.6 broadcast_multiply_fusion
  (5 shorter events, 0.0 us)
Async XLA Ops:
  2.6 44.2 %copy-start = (bf16[256,64]{0,1:T(8,128)(2,1)S(1)}, bf16[256,64]{0,1:T(8,128)(2,1)}, u32[]{:S(2)}) copy-start(bf16[256,64]{0,1:T(8,128)(2,1)} %param.17) | copy-start | bytes 98308
  56.7 21.8 %collective-permute-start.4 = (f32[8,2,128]{2,1,0:T(2,128)S(1)}, f32[8,2,128]{2,1,0:T(2,128)S(1)}, u32[]{:S(2)}, u32[]{:S(2)}) collective-permute-start(f32[8,2,128]{2,1,0:T(2,128)S(1)} %get-tuple-element.87), channel_id=1, source_target_pairs={{496,48},{497,49},{498,50},{499,51},{500,52},{501,53},{502,54},{50... | collective-permute-start | bytes 24584 | tf_op jit(solution)/shard_map/ppermute | solution.py:207
  57.4 21.2 %collective-permute-start.5 = (f32[8,2,128]{2,1,0:T(2,128)S(1)}, f32[8,2,128]{2,1,0:T(2,128)S(1)}, u32[]{:S(2)}, u32[]{:S(2)}) collective-permute-start(f32[8,2,128]{2,1,0:T(2,128)S(1)} %get-tuple-element.88), channel_id=1, source_target_pairs={{496,176},{497,177},{498,178},{499,179},{500,180},{501,181},{502,1... | collective-permute-start | bytes 24584 | tf_op jit(solution)/shard_map/ppermute | solution.py:207
  58.1 20.5 %collective-permute-start.6 = (f32[8,2,128]{2,1,0:T(2,128)S(1)}, f32[8,2,128]{2,1,0:T(2,128)S(1)}, u32[]{:S(2)}, u32[]{:S(2)}) collective-permute-start(f32[8,2,128]{2,1,0:T(2,128)S(1)} %get-tuple-element.89), channel_id=1, source_target_pairs={{496,304},{497,305},{498,306},{499,307},{500,308},{501,309},{502,3... | collective-permute-start | bytes 24584 | tf_op jit(solution)/shard_map/ppermute | solution.py:207
  58.7 19.8 %collective-permute-start.7 = (f32[8,2,128]{2,1,0:T(2,128)S(1)}, f32[8,2,128]{2,1,0:T(2,128)S(1)}, u32[]{:S(2)}, u32[]{:S(2)}) collective-permute-start(f32[8,2,128]{2,1,0:T(2,128)S(1)} %get-tuple-element.90), channel_id=1, source_target_pairs={{496,432},{497,433},{498,434},{499,435},{500,436},{501,437},{502,4... | collective-permute-start | bytes 24584 | tf_op jit(solution)/shard_map/ppermute | solution.py:207
  59.4 36.6 %copy-start.1 = (f32[2,128]{1,0:T(2,128)S(1)}, f32[2,128]{1,0:T(2,128)}, u32[]{:S(2)}) copy-start(f32[2,128]{1,0:T(2,128)} %param.15) | copy-start | bytes 3076
  59.4 36.6 %copy-start.2 = (f32[2,128]{1,0:T(2,128)S(1)}, f32[2,128]{1,0:T(2,128)}, u32[]{:S(2)}) copy-start(f32[2,128]{1,0:T(2,128)} %param.16) | copy-start | bytes 3076
  79.7 0.7 collective-permute-start
  80.4 2.7 %collective-permute-start.2 = (f32[2,128]{1,0:T(2,128)S(1)}, f32[2,128]{1,0:T(2,128)S(1)}, u32[]{:S(2)}, u32[]{:S(2)}) collective-permute-start(f32[2,128]{1,0:T(2,128)S(1)} %get-tuple-element.97), channel_id=1, source_target_pairs={{48,16},{112,80},{176,144},{240,208},{304,272},{368,336},{432,400}... | collective-permute-start | bytes 3080 | tf_op jit(solution)/shard_map/cond/branch_0_fun/ppermute | solution.py:227
  81.0 15.0 %collective-permute-start.1 = (f32[2,128]{1,0:T(2,128)S(1)}, f32[2,128]{1,0:T(2,128)S(1)}, u32[]{:S(2)}, u32[]{:S(2)}) collective-permute-start(f32[2,128]{1,0:T(2,128)S(1)} %get-tuple-element.98), channel_id=1, source_target_pairs={{48,0},{112,64},{176,128},{240,192},{304,256},{368,320},{432,384},... | collective-permute-start | bytes 3080 | tf_op jit(solution)/shard_map/cond/branch_0_fun/ppermute | solution.py:227
  82.3 13.7 %collective-permute-start.3 = (f32[2,128]{1,0:T(2,128)S(1)}, f32[2,128]{1,0:T(2,128)S(1)}, u32[]{:S(2)}, u32[]{:S(2)}) collective-permute-start(f32[2,128]{1,0:T(2,128)S(1)} %get-tuple-element.99), channel_id=1, source_target_pairs={{48,32},{112,96},{176,160},{240,224},{304,288},{368,352},{432,416}... | collective-permute-start | bytes 3080 | tf_op jit(solution)/shard_map/cond/branch_0_fun/ppermute | solution.py:227

commit v5 on v4

--- a/solution.py
+++ b/solution.py
@@ -9,7 +9,9 @@
 
 HD = 128
 BLOCK = 256
-NEAR = 8
+RUNS = (8, 8, 16)
+ORDER = (1, 2, 0)
+SENDS = (1, 2, 3)
 
 alpha_now = 0.6
 sigma_now = 0.8
@@ -124,9 +126,9 @@
     )(blocks, weight)
 
 
-def noise_shapes_of(comp_count, own, tokens):
-    run = jax.ShapeDtypeStruct((NEAR, own, tokens), jnp.float32)
-    return [run] * (comp_count // NEAR) + [jax.ShapeDtypeStruct((own, tokens), jnp.float32)]
+def noise_shapes_of(own, tokens):
+    runs = [jax.ShapeDtypeStruct((run, own, tokens), jnp.float32) for run in RUNS]
+    return [*runs, jax.ShapeDtypeStruct((own, tokens), jnp.float32)]
 
 
 def noise_parts(returned, width, noise_shapes):
@@ -140,10 +142,11 @@
             total += in_ref[d].astype(jnp.float32)
         squares = total[channels : channels + 1] + total[channels + 8 : channels + 9]
         noise = total[:channels] / jnp.sqrt(squares / width + 1e-06)
-        for r, out_ref in enumerate(out_refs[:-1]):
-            for n in range(NEAR):
-                start = (r * NEAR + n) * own
+        start = 0
+        for run, out_ref in zip(RUNS, out_refs):
+            for n in range(run):
                 out_ref[n] = noise[start : start + own]
+                start += own
         out_refs[-1][...] = noise[channels - own :]
 
     return pl.pallas_call(
@@ -184,9 +187,8 @@
     blocks = lax.all_to_all(packed, "seq", split_axis=0, concat_axis=0, tiled=True)
     own = latent.shape[0]
     width = queries.shape[2]
-    noise_shapes = noise_shapes_of(comp_count, own, tokens)
-    half = NEAR // 2
-    runs = [list(range(first, first + NEAR)) for first in range(0, comp_count, NEAR)]
+    noise_shapes = noise_shapes_of(own, tokens)
+    firsts = [sum(RUNS[:r]) for r in range(len(RUNS))]
 
     def exchange(array):
         return lax.all_to_all(array, "seq", split_axis=0, concat_axis=0, tiled=True)
@@ -204,32 +206,26 @@
 
     blocks, comp = lax.optimization_barrier((blocks, comp))
     outputs, *noise = lax.cond(comp == last, on_last, elsewhere, blocks, head_weight.T)
-    sent = [lax.ppermute(noise[r], "comp", [(last, run[half - 1])]) for r, run in enumerate(runs)]
+    sent = {r: lax.ppermute(noise[r], "comp", [(last, firsts[r])]) for r in ORDER}
     returned = lax.cond(comp == last, exchange, exchange_grouped, outputs)
-    returned, sent = lax.optimization_barrier((returned, sent))
     hidden = assemble(returned)
-    part = sum(sent[1:], sent[0])
-
-    def own_of_last(part):
+    hidden, sent = lax.optimization_barrier((hidden, sent))
+
+    def own_of_last(sent):
         return noise[-1]
 
-    def from_holders(part):
-        holders = [(run[half - 1], run[-1] if run[-1] != last else run[-2]) for run in runs]
-        passed = lax.ppermute(part[half:], "comp", holders)
-        held = jnp.where(comp % NEAR == half - 1, part[:half], passed)
-        result = jnp.zeros((own, tokens), jnp.float32)
-        for n in range(half):
-            pairs = []
-            for run, (first, second) in zip(runs, holders):
-                pairs += [(first, run[n]), (second, run[half + n])]
-            pairs = [(source, target) for source, target in pairs if target not in (source, last)]
-            if pairs:
-                result += lax.ppermute(held[n], "comp", pairs)
-        kept = (comp % NEAR == half - 1) | (comp % NEAR == NEAR - 1)
-        result = jnp.where(kept, held[half - 1], result)
-        return jnp.where(comp == last - 1, held[half - 2], result)
-
-    noise_own = lax.cond(comp == last, own_of_last, from_holders, part)
+    def from_holders(sent):
+        pairs = [(firsts[2], firsts[2] + 8)]
+        held = sent[0] + sent[1] + sent[2][:8] + lax.ppermute(sent[2][8:], "comp", pairs)
+        pairs = [(c, c + 4) for c in range(0, comp_count, 8)]
+        held = held[:4] + lax.ppermute(held[4:], "comp", pairs)
+        result = held[0]
+        for n in SENDS:
+            pairs = [(c, c + n) for c in range(0, comp_count, 4) if c + n != last]
+            result += lax.ppermute(held[n], "comp", pairs)
+        return result
+
+    noise_own = lax.cond(comp == last, own_of_last, from_holders, sent)
     denoised = (latent - sigma_now * noise_own) / alpha_now
     step_now = math.log(alpha_next / sigma_next) - math.log(alpha_now / sigma_now)
     ratio = step_before / step_now

time: 97 us -> 94.9 us (0.978)
  the two profiles are of different devices: /device:TPU:448 before, /device:TPU:32 now
where the time goes in v5:
time: 94.9 us; the launch traced here: 94.5 us
  blocking collectives  62.4 us (66%)
  Pallas kernels  12.7 us (13%)
  waiting for transfers between devices  11.7 us (12%)
  starting transfers between devices  5.92 us (6%)
    all_to_all x1, blocking collectives, on_device(): lax.all_to_all(packed, 'seq', split_axis=0, concat_axis=0, tiled=True)  43.3 us
    all_to_all x1, blocking collectives, exchange_grouped(): lax.all_to_all(array, 'seq', split_axis=0, concat_axis=0, tiled=True, axi...  19.1 us
    ppermute x3, waiting for transfers between devices, from_holders(): result += lax.ppermute(held[n], 'comp', pairs)  11.7 us
    pallas_call x1, Pallas kernels, attention(): pl.pallas_call(kernel, out_shape=[jax.ShapeDtypeStruct((seq_count, tokens...  9.75 us
    ppermute x3, starting transfers between devices, from_holders(): result += lax.ppermute(held[n], 'comp', pairs)  2.62 us
    ppermute x3, starting transfers between devices, on_device(): lax.ppermute(noise[r], 'comp', [(last, firsts[r])])  1.99 us
    pallas_call x1, Pallas kernels, pack(): pl.pallas_call(kernel, out_shape=jax.ShapeDtypeStruct((seq_count, 3, toke...  1.92 us
  transfers between devices with their start and end apart: 8, of which 1 were waited for; matrix products, arithmetic and copies ran while one was open for 0% of the time, Pallas kernels for 1%

profile of v5, /device:TPU:32, one launch (start us, length us, event | category | flops | bytes accessed | tf_op | source)
XLA Modules:
  0.0 94.5 jit_solution(5161733168636086520)
XLA Ops:
  0.6 1.9 %pack.1 = bf16[16,3,128,256]{3,2,1,0:T(8,128)(2,1)S(1)} custom-call(bf16[128,4096]{1,0:T(8,128)(2,1)} %bitcast.20, bf16[128,4096]{1,0:T(8,128)(2,1)} %bitcast.21, bf16[128,4096]{1,0:T(8,128)(2,1)} %bitcast.22), custom_call_target="tpu_custom_call" | custom-call | tf_op jit(solution)/shard_map/pack/pallas_call | solution.py:50
  2.6 0.0 copy-start
  2.6 43.3 %all_to_all.20 = bf16[16,3,128,256]{3,2,1,0:T(8,128)(2,1)S(1)} all-to-all(bf16[16,3,128,256]{3,2,1,0:T(8,128)(2,1)S(1)} %pack.1), channel_id=1, replica_groups=mesh['comp'=32,'seq'=16] {'seq'}, dimensions={0} | all-to-all | bytes 6291456 | tf_op jit(solution)/shard_map/all_to_all | solution.py:187
  45.8 0.0 copy-done
  45.8 10.0 %conditional.3 = (f32[8,2,128]{2,1,0:T(2,128)S(1)}, f32[8,2,128]{2,1,0:T(2,128)S(1)}, f32[16,2,128]{2,1,0:T(2,128)S(1)}, bf16[16,128,256]{2,1,0:T(8,128)(2,1)S(1)}, f32[2,128]{1,0:T(2,128)S(1)}) conditional(s32[]{:T(128)} %convert_element_type.2, (bf16[16,3,128,256]{3,2,1,0:T(8,128)(2,1)S(1)}, bf16[64,256]{1,0:T(8,128)(2,1)S(1)}) %tuple.54, ...), branch_computations={%region_0.0_spmd, %region_1.0_spmd} | conditional | bytes 655400 | solution.py:208
  45.8 9.8 %attention.2 = (bf16[16,128,256]{2,1,0:T(8,128)(2,1)S(1)}, f32[8,2,128]{2,1,0:T(2,128)S(1)}, f32[8,2,128]{2,1,0:T(2,128)S(1)}, f32[16,2,128]{2,1,0:T(2,128)S(1)}, f32[2,128]{1,0:T(2,128)S(1)}) custom-call(bf16[16,3,128,256]{3,2,1,0:T(8,128)(2,1)S(1)} %get-tuple-element.30.in_ref, bf16[64,256]{1,0:T(8,128)(2,1)S(1)} %get-tuple-element.31.weight_ref), custom_call_target="tpu_custom_call" | custom-call | tf_op jit(solution)/shard_map/cond/branch_0_fun/attention/pallas_call | solution.py:119
  55.8 0.7 collective-permute-start.7
  56.5 0.7 collective-permute-start.5
  57.2 0.7 collective-permute-start.6
  57.8 0.0 copy-start.1
  57.9 0.0 copy-start.2
  57.9 19.1 %conditional.4 = (bf16[16,128,256]{2,1,0:T(8,128)(2,1)S(1)}) conditional(s32[]{:T(128)} %convert_element_type.2, bf16[16,128,256]{2,1,0:T(8,128)(2,1)S(1)} %get-tuple-element.72, bf16[16,128,256]{2,1,0:T(8,128)(2,1)S(1)} %get-tuple-element.72), branch_computations={%region_2.0_spmd, %region_3.0_spmd} | conditional | bytes 2097160 | solution.py:210
  57.9 19.1 %all_to_all.18 = bf16[16,128,256]{2,1,0:T(8,128)(2,1)S(1)} all-to-all(bf16[16,128,256]{2,1,0:T(8,128)(2,1)S(1)} %param.2), channel_id=1, replica_groups={{0,1,2,3,4,5,6,7,8,9,10,11,12,13,14,15},{16,17,18,19,20,21,22,23,24,25,..., dimensions={0} | all-to-all | bytes 2097152 | tf_op jit(solution)/shard_map/cond/branch_0_fun/all_to_all | solution.py:198
  77.0 1.1 %assemble.1 = bf16[128,4096]{1,0:T(8,128)(2,1)} custom-call(bf16[16,128,256]{2,1,0:T(8,128)(2,1)S(1)} %get-tuple-element.96.in_ref), custom_call_target="tpu_custom_call" | custom-call | tf_op jit(solution)/shard_map/assemble/pallas_call | solution.py:169
  78.1 0.0 collective-permute-done.5
  78.1 0.0 collective-permute-done.6
  78.1 0.0 collective-permute-done.7
  78.1 15.8 %conditional.5 = (f32[2,128]{1,0:T(2,128)S(1)}) conditional(s32[]{:T(128)} %convert_element_type.2, (f32[8,2,128]{2,1,0:T(2,128)S(1)}, f32[8,2,128]{2,1,0:T(2,128)S(1)}, f32[16,2,128]{2,1,0:T(2,128)S(1)}) %tuple.43, f32[2,128]{1,0:T(2,128)S(1)} %get-tuple-element.80), branch_computations={%region_4.0_spmd, %region_5.0_spmd} | conditional | flops 7936 | bytes 150736 | solution.py:228
  78.1 0.7 collective-permute-start
  78.8 0.0 collective-permute-done
  78.8 0.7 collective-permute-start.1
  79.5 0.0 collective-permute-done.1
  79.5 0.7 collective-permute-start.2
  80.2 0.7 collective-permute-start.4
  80.9 1.3 %collective-permute-start.3 = (f32[2,128]{1,0:T(2,128)S(1)}, f32[2,128]{1,0:T(2,128)S(1)}, u32[]{:S(2)}, u32[]{:S(2)}) collective-permute-start(f32[2,128]{1,0:T(2,128)S(1)} %get-tuple-element.83), channel_id=1, source_target_pairs={{0,32},{64,96},{128,160},{192,224},{256,288},{320,352},{384,416},{... | collective-permute-start | bytes 3080 | tf_op jit(solution)/shard_map/cond/branch_0_fun/ppermute | solution.py:225
  82.2 0.0 collective-permute-done.2
  82.2 0.0 collective-permute-done.4
  82.2 11.7 %collective-permute-done.3 = f32[2,128]{1,0:T(2,128)S(1)} collective-permute-done((f32[2,128]{1,0:T(2,128)S(1)}, f32[2,128]{1,0:T(2,128)S(1)}, u32[]{:S(2)}, u32[]{:S(2)}) %collective-permute-start.3) | collective-permute-done | bytes 1056 | tf_op jit(solution)/shard_map/cond/branch_0_fun/ppermute | solution.py:225
  93.9 0.0 copy-done.1
  93.9 0.0 copy-done.2
  93.9 0.6 broadcast_multiply_fusion
  (6 shorter events, 0.0 us)
Async XLA Ops:
  2.6 43.3 %copy-start = (bf16[256,64]{0,1:T(8,128)(2,1)S(1)}, bf16[256,64]{0,1:T(8,128)(2,1)}, u32[]{:S(2)}) copy-start(bf16[256,64]{0,1:T(8,128)(2,1)} %param.17) | copy-start | bytes 98308
  55.8 22.2 %collective-permute-start.7 = (f32[16,2,128]{2,1,0:T(2,128)S(1)}, f32[16,2,128]{2,1,0:T(2,128)S(1)}, u32[]{:S(2)}, u32[]{:S(2)}) collective-permute-start(f32[16,2,128]{2,1,0:T(2,128)S(1)} %get-tuple-element.75), channel_id=1, source_target_pairs={{496,256},{497,257},{498,258},{499,259},{500,260},{501,261},{502,2... | collective-permute-start | bytes 49160 | tf_op jit(solution)/shard_map/ppermute | solution.py:209
  56.5 21.6 %collective-permute-start.5 = (f32[8,2,128]{2,1,0:T(2,128)S(1)}, f32[8,2,128]{2,1,0:T(2,128)S(1)}, u32[]{:S(2)}, u32[]{:S(2)}) collective-permute-start(f32[8,2,128]{2,1,0:T(2,128)S(1)} %get-tuple-element.73), channel_id=1, source_target_pairs={{496,0},{497,1},{498,2},{499,3},{500,4},{501,5},{502,6},{503,7},{5... | collective-permute-start | bytes 24584 | tf_op jit(solution)/shard_map/ppermute | solution.py:209
  57.2 20.9 %collective-permute-start.6 = (f32[8,2,128]{2,1,0:T(2,128)S(1)}, f32[8,2,128]{2,1,0:T(2,128)S(1)}, u32[]{:S(2)}, u32[]{:S(2)}) collective-permute-start(f32[8,2,128]{2,1,0:T(2,128)S(1)} %get-tuple-element.74), channel_id=1, source_target_pairs={{496,128},{497,129},{498,130},{499,131},{500,132},{501,133},{502,1... | collective-permute-start | bytes 24584 | tf_op jit(solution)/shard_map/ppermute | solution.py:209
  57.8 36.1 %copy-start.1 = (f32[2,128]{1,0:T(2,128)S(1)}, f32[2,128]{1,0:T(2,128)}, u32[]{:S(2)}) copy-start(f32[2,128]{1,0:T(2,128)} %param.15) | copy-start | bytes 3076
  57.9 36.1 %copy-start.2 = (f32[2,128]{1,0:T(2,128)S(1)}, f32[2,128]{1,0:T(2,128)}, u32[]{:S(2)}) copy-start(f32[2,128]{1,0:T(2,128)} %param.16) | copy-start | bytes 3076
  78.1 0.7 collective-permute-start
  78.8 0.7 collective-permute-start.1
  79.5 2.6 %collective-permute-start.2 = (f32[2,128]{1,0:T(2,128)S(1)}, f32[2,128]{1,0:T(2,128)S(1)}, u32[]{:S(2)}, u32[]{:S(2)}) collective-permute-start(f32[2,128]{1,0:T(2,128)S(1)} %get-tuple-element.81), channel_id=1, source_target_pairs={{0,16},{64,80},{128,144},{192,208},{256,272},{320,336},{384,400},{... | collective-permute-start | bytes 3080 | tf_op jit(solution)/shard_map/cond/branch_0_fun/ppermute | solution.py:225
  80.2 2.0 %collective-permute-start.4 = (f32[2,128]{1,0:T(2,128)S(1)}, f32[2,128]{1,0:T(2,128)S(1)}, u32[]{:S(2)}, u32[]{:S(2)}) collective-permute-start(f32[2,128]{1,0:T(2,128)S(1)} %get-tuple-element.82), channel_id=1, source_target_pairs={{0,48},{64,112},{128,176},{192,240},{256,304},{320,368},{384,432},... | collective-permute-start | bytes 3080 | tf_op jit(solution)/shard_map/cond/branch_0_fun/ppermute | solution.py:225
  80.9 13.0 %collective-permute-start.3 = (f32[2,128]{1,0:T(2,128)S(1)}, f32[2,128]{1,0:T(2,128)S(1)}, u32[]{:S(2)}, u32[]{:S(2)}) collective-permute-start(f32[2,128]{1,0:T(2,128)S(1)} %get-tuple-element.83), channel_id=1, source_target_pairs={{0,32},{64,96},{128,160},{192,224},{256,288},{320,352},{384,416},{... | collective-permute-start | bytes 3080 | tf_op jit(solution)/shard_map/cond/branch_0_fun/ppermute | solution.py:225

commit v6 on v5

--- a/solution.py
+++ b/solution.py
@@ -8,7 +8,7 @@
 from jax.sharding import PartitionSpec as P
 
 HD = 128
-BLOCK = 256
+BLOCK = 512
 RUNS = (8, 8, 16)
 ORDER = (1, 2, 0)
 SENDS = (1, 2, 3)

time: 94.9 us -> 94.8 us (level)
  no operation moved by 1% of the time
where the time goes in v6:
time: 94.8 us; the launch traced here: 94.4 us
  blocking collectives  62.4 us (66%)
  Pallas kernels  12.6 us (13%)
  waiting for transfers between devices  11.8 us (12%)
  starting transfers between devices  5.92 us (6%)
    all_to_all x1, blocking collectives, on_device(): lax.all_to_all(packed, 'seq', split_axis=0, concat_axis=0, tiled=True)  43.3 us
    all_to_all x1, blocking collectives, exchange_grouped(): lax.all_to_all(array, 'seq', split_axis=0, concat_axis=0, tiled=True, axi...  19.1 us
    ppermute x3, waiting for transfers between devices, from_holders(): result += lax.ppermute(held[n], 'comp', pairs)  11.8 us
    pallas_call x1, Pallas kernels, attention(): pl.pallas_call(kernel, out_shape=[jax.ShapeDtypeStruct((seq_count, tokens...  9.59 us
    ppermute x3, starting transfers between devices, from_holders(): result += lax.ppermute(held[n], 'comp', pairs)  2.62 us
    ppermute x3, starting transfers between devices, on_device(): lax.ppermute(noise[r], 'comp', [(last, firsts[r])])  1.99 us
    pallas_call x1, Pallas kernels, pack(): pl.pallas_call(kernel, out_shape=jax.ShapeDtypeStruct((seq_count, 3, toke...  1.92 us
  transfers between devices with their start and end apart: 8, of which 1 were waited for; matrix products, arithmetic and copies ran while one was open for 0% of the time, Pallas kernels for 1%

profile of v6, /device:TPU:32, one launch (start us, length us, event | category | flops | bytes accessed | tf_op | source)
XLA Modules:
  0.0 94.4 jit_solution(7740337285762324189)
XLA Ops:
  0.6 1.9 %pack.1 = bf16[16,3,128,256]{3,2,1,0:T(8,128)(2,1)S(1)} custom-call(bf16[128,4096]{1,0:T(8,128)(2,1)} %bitcast.20, bf16[128,4096]{1,0:T(8,128)(2,1)} %bitcast.21, bf16[128,4096]{1,0:T(8,128)(2,1)} %bitcast.22), custom_call_target="tpu_custom_call" | custom-call | tf_op jit(solution)/shard_map/pack/pallas_call | solution.py:50
  2.6 0.0 copy-start
  2.6 43.3 %all_to_all.20 = bf16[16,3,128,256]{3,2,1,0:T(8,128)(2,1)S(1)} all-to-all(bf16[16,3,128,256]{3,2,1,0:T(8,128)(2,1)S(1)} %pack.1), channel_id=1, replica_groups=mesh['comp'=32,'seq'=16] {'seq'}, dimensions={0} | all-to-all | bytes 6291456 | tf_op jit(solution)/shard_map/all_to_all | solution.py:187
  45.8 0.0 copy-done
  45.8 9.8 %conditional.3 = (f32[8,2,128]{2,1,0:T(2,128)S(1)}, f32[8,2,128]{2,1,0:T(2,128)S(1)}, f32[16,2,128]{2,1,0:T(2,128)S(1)}, bf16[16,128,256]{2,1,0:T(8,128)(2,1)S(1)}, f32[2,128]{1,0:T(2,128)S(1)}) conditional(s32[]{:T(128)} %convert_element_type.2, (bf16[16,3,128,256]{3,2,1,0:T(8,128)(2,1)S(1)}, bf16[64,256]{1,0:T(8,128)(2,1)S(1)}) %tuple.54, ...), branch_computations={%region_0.0_spmd, %region_1.0_spmd} | conditional | bytes 655400 | solution.py:208
  45.8 9.6 %attention.2 = (bf16[16,128,256]{2,1,0:T(8,128)(2,1)S(1)}, f32[8,2,128]{2,1,0:T(2,128)S(1)}, f32[8,2,128]{2,1,0:T(2,128)S(1)}, f32[16,2,128]{2,1,0:T(2,128)S(1)}, f32[2,128]{1,0:T(2,128)S(1)}) custom-call(bf16[16,3,128,256]{3,2,1,0:T(8,128)(2,1)S(1)} %get-tuple-element.30.in_ref, bf16[64,256]{1,0:T(8,128)(2,1)S(1)} %get-tuple-element.31.weight_ref), custom_call_target="tpu_custom_call" | custom-call | tf_op jit(solution)/shard_map/cond/branch_0_fun/attention/pallas_call | solution.py:119
  55.7 0.7 collective-permute-start.7
  56.3 0.7 collective-permute-start.5
  57.0 0.7 collective-permute-start.6
  57.7 0.0 copy-start.1
  57.7 0.0 copy-start.2
  57.7 19.1 %conditional.4 = (bf16[16,128,256]{2,1,0:T(8,128)(2,1)S(1)}) conditional(s32[]{:T(128)} %convert_element_type.2, bf16[16,128,256]{2,1,0:T(8,128)(2,1)S(1)} %get-tuple-element.72, bf16[16,128,256]{2,1,0:T(8,128)(2,1)S(1)} %get-tuple-element.72), branch_computations={%region_2.0_spmd, %region_3.0_spmd} | conditional | bytes 2097160 | solution.py:210
  57.7 19.1 %all_to_all.18 = bf16[16,128,256]{2,1,0:T(8,128)(2,1)S(1)} all-to-all(bf16[16,128,256]{2,1,0:T(8,128)(2,1)S(1)} %param.2), channel_id=1, replica_groups={{0,1,2,3,4,5,6,7,8,9,10,11,12,13,14,15},{16,17,18,19,20,21,22,23,24,25,..., dimensions={0} | all-to-all | bytes 2097152 | tf_op jit(solution)/shard_map/cond/branch_0_fun/all_to_all | solution.py:198
  76.8 1.1 %assemble.1 = bf16[128,4096]{1,0:T(8,128)(2,1)} custom-call(bf16[16,128,256]{2,1,0:T(8,128)(2,1)S(1)} %get-tuple-element.96.in_ref), custom_call_target="tpu_custom_call" | custom-call | tf_op jit(solution)/shard_map/assemble/pallas_call | solution.py:169
  77.9 0.0 collective-permute-done.5
  77.9 0.0 collective-permute-done.6
  77.9 0.0 collective-permute-done.7
  77.9 15.9 %conditional.5 = (f32[2,128]{1,0:T(2,128)S(1)}) conditional(s32[]{:T(128)} %convert_element_type.2, (f32[8,2,128]{2,1,0:T(2,128)S(1)}, f32[8,2,128]{2,1,0:T(2,128)S(1)}, f32[16,2,128]{2,1,0:T(2,128)S(1)}) %tuple.43, f32[2,128]{1,0:T(2,128)S(1)} %get-tuple-element.80), branch_computations={%region_4.0_spmd, %region_5.0_spmd} | conditional | flops 7936 | bytes 150736 | solution.py:228
  77.9 0.7 collective-permute-start
  78.6 0.0 collective-permute-done
  78.6 0.7 collective-permute-start.1
  79.3 0.0 collective-permute-done.1
  79.4 0.7 collective-permute-start.2
  80.0 0.7 collective-permute-start.4
  80.7 1.3 %collective-permute-start.3 = (f32[2,128]{1,0:T(2,128)S(1)}, f32[2,128]{1,0:T(2,128)S(1)}, u32[]{:S(2)}, u32[]{:S(2)}) collective-permute-start(f32[2,128]{1,0:T(2,128)S(1)} %get-tuple-element.83), channel_id=1, source_target_pairs={{0,32},{64,96},{128,160},{192,224},{256,288},{320,352},{384,416},{... | collective-permute-start | bytes 3080 | tf_op jit(solution)/shard_map/cond/branch_0_fun/ppermute | solution.py:225
  82.0 0.0 collective-permute-done.2
  82.0 0.0 collective-permute-done.4
  82.0 11.8 %collective-permute-done.3 = f32[2,128]{1,0:T(2,128)S(1)} collective-permute-done((f32[2,128]{1,0:T(2,128)S(1)}, f32[2,128]{1,0:T(2,128)S(1)}, u32[]{:S(2)}, u32[]{:S(2)}) %collective-permute-start.3) | collective-permute-done | bytes 1056 | tf_op jit(solution)/shard_map/cond/branch_0_fun/ppermute | solution.py:225
  93.8 0.0 copy-done.1
  93.8 0.0 copy-done.2
  93.8 0.6 broadcast_multiply_fusion
  (6 shorter events, 0.0 us)
Async XLA Ops:
  2.6 43.3 %copy-start = (bf16[256,64]{0,1:T(8,128)(2,1)S(1)}, bf16[256,64]{0,1:T(8,128)(2,1)}, u32[]{:S(2)}) copy-start(bf16[256,64]{0,1:T(8,128)(2,1)} %param.17) | copy-start | bytes 98308
  55.7 22.2 %collective-permute-start.7 = (f32[16,2,128]{2,1,0:T(2,128)S(1)}, f32[16,2,128]{2,1,0:T(2,128)S(1)}, u32[]{:S(2)}, u32[]{:S(2)}) collective-permute-start(f32[16,2,128]{2,1,0:T(2,128)S(1)} %get-tuple-element.75), channel_id=1, source_target_pairs={{496,256},{497,257},{498,258},{499,259},{500,260},{501,261},{502,2... | collective-permute-start | bytes 49160 | tf_op jit(solution)/shard_map/ppermute | solution.py:209
  56.3 21.6 %collective-permute-start.5 = (f32[8,2,128]{2,1,0:T(2,128)S(1)}, f32[8,2,128]{2,1,0:T(2,128)S(1)}, u32[]{:S(2)}, u32[]{:S(2)}) collective-permute-start(f32[8,2,128]{2,1,0:T(2,128)S(1)} %get-tuple-element.73), channel_id=1, source_target_pairs={{496,0},{497,1},{498,2},{499,3},{500,4},{501,5},{502,6},{503,7},{5... | collective-permute-start | bytes 24584 | tf_op jit(solution)/shard_map/ppermute | solution.py:209
  57.0 20.9 %collective-permute-start.6 = (f32[8,2,128]{2,1,0:T(2,128)S(1)}, f32[8,2,128]{2,1,0:T(2,128)S(1)}, u32[]{:S(2)}, u32[]{:S(2)}) collective-permute-start(f32[8,2,128]{2,1,0:T(2,128)S(1)} %get-tuple-element.74), channel_id=1, source_target_pairs={{496,128},{497,129},{498,130},{499,131},{500,132},{501,133},{502,1... | collective-permute-start | bytes 24584 | tf_op jit(solution)/shard_map/ppermute | solution.py:209
  57.7 36.1 %copy-start.1 = (f32[2,128]{1,0:T(2,128)S(1)}, f32[2,128]{1,0:T(2,128)}, u32[]{:S(2)}) copy-start(f32[2,128]{1,0:T(2,128)} %param.15) | copy-start | bytes 3076
  57.7 36.1 %copy-start.2 = (f32[2,128]{1,0:T(2,128)S(1)}, f32[2,128]{1,0:T(2,128)}, u32[]{:S(2)}) copy-start(f32[2,128]{1,0:T(2,128)} %param.16) | copy-start | bytes 3076
  77.9 0.7 collective-permute-start
  78.6 0.7 collective-permute-start.1
  79.4 2.6 %collective-permute-start.2 = (f32[2,128]{1,0:T(2,128)S(1)}, f32[2,128]{1,0:T(2,128)S(1)}, u32[]{:S(2)}, u32[]{:S(2)}) collective-permute-start(f32[2,128]{1,0:T(2,128)S(1)} %get-tuple-element.81), channel_id=1, source_target_pairs={{0,16},{64,80},{128,144},{192,208},{256,272},{320,336},{384,400},{... | collective-permute-start | bytes 3080 | tf_op jit(solution)/shard_map/cond/branch_0_fun/ppermute | solution.py:225
  80.0 2.0 %collective-permute-start.4 = (f32[2,128]{1,0:T(2,128)S(1)}, f32[2,128]{1,0:T(2,128)S(1)}, u32[]{:S(2)}, u32[]{:S(2)}) collective-permute-start(f32[2,128]{1,0:T(2,128)S(1)} %get-tuple-element.82), channel_id=1, source_target_pairs={{0,48},{64,112},{128,176},{192,240},{256,304},{320,368},{384,432},... | collective-permute-start | bytes 3080 | tf_op jit(solution)/shard_map/cond/branch_0_fun/ppermute | solution.py:225
  80.7 13.1 %collective-permute-start.3 = (f32[2,128]{1,0:T(2,128)S(1)}, f32[2,128]{1,0:T(2,128)S(1)}, u32[]{:S(2)}, u32[]{:S(2)}) collective-permute-start(f32[2,128]{1,0:T(2,128)S(1)} %get-tuple-element.83), channel_id=1, source_target_pairs={{0,32},{64,96},{128,160},{192,224},{256,288},{320,352},{384,416},{... | collective-permute-start | bytes 3080 | tf_op jit(solution)/shard_map/cond/branch_0_fun/ppermute | solution.py:225
